TPU v7x, 256 devices: a whole 4x4x8 slice. The times are simulated.
256 devices in a mesh: grp: 2 (over z_hi), row: 4 (over y), tp: 32 (over z_lo, x, core).
Axes of the slice: x: 4, y: 4, z: 8 (z_hi: 2, z_lo: 4; z = z_hi * 4 + z_lo), core: 2. Of those that a mesh axis runs over, the one named last changes fastest.
Arguments:
- query: bfloat16 [32, 16384], P(('grp', 'row')), may hold values from -120 to 120
- cached_key_rows: bfloat16 [32, 8192, 1024], P(('grp', 'row'), 'tp'), may hold values from -6 to 6
- cached_value_rows: bfloat16 [32, 8192, 1024], P(('grp', 'row'), 'tp'), may hold values from -6 to 6
- row_cache_length: int32 [32], P(('grp', 'row')), may hold values from 2 to 8192, as said below
- attention_output_weight: bfloat16 [16384, 16384], P('tp', 'row'), may hold values from -1.5 to 1.5
- resid: bfloat16 [32, 16384], P('grp', ('row', 'tp')), may hold values from -16 to 16
- feed_norm_scale: bfloat16 [16384], P(('row', 'tp')), may hold values from 0.5 to 1.5
- gate_down_weight: bfloat16 [16384, 1024], P(('row', 'tp')), may hold values from -0.046875 to 0.046875
- up_down_weight: bfloat16 [16384, 1024], P(('row', 'tp')), may hold values from -0.046875 to 0.046875
- gate_expansion_weight: bfloat16 [1024, 53248], P('grp', 'tp'), may hold values from -1.5 to 1.5
- up_expansion_weight: bfloat16 [1024, 53248], P('grp', 'tp'), may hold values from -1.5 to 1.5
- row_adapter_index: int32 [32], replicated, may hold values from 0 to 63
Outputs:
- stream: bfloat16 [32, 16384], P('grp', ('row', 'tp'))
- gate_delta: bfloat16 [32, 53248], P(('grp', 'row'), 'tp')
- up_delta: bfloat16 [32, 53248], P(('grp', 'row'), 'tp')
Inputs may be any that keep to these rules, and one draw needn't show every extreme that they name: `row_cache_length`: some row has all 8192 positions live.
All inputs are finite; a program needn't handle non-finite values.
Results may differ from a plain program's by a relative error of at most 0.011.
Values may be sent and summed in bfloat16 or wider, within the bound.
A program may use at most 128 MiB of HBM per device.

v0:
```python
import jax
import jax.numpy as jnp
from jax import lax
from jax.sharding import PartitionSpec as P

MODEL_WIDTH = 16384
HQ = 128
KVH = 8
HD = 128
ADAPTER_RANK = 16
ADAPTER_COUNT = 64


epsilon = 1e-05


def joined(part, axis, combine):
    gathered = jax.tree.map(lambda a: lax.all_gather(a, axis), part)

    def take(source):
        return jax.tree.map(lambda a: lax.dynamic_index_in_dim(a, source, 0, False), gathered)

    return lax.fori_loop(
        1, lax.axis_size(axis), lambda source, state: combine(state, take(source)), take(0)
    )


def combine_parts(earlier, latter):
    high_one, total_one, accum_one = earlier
    high_two, total_two, accum_two = latter
    highest = jnp.maximum(high_one, high_two)
    factor_one = jnp.exp(high_one - highest)
    factor_two = jnp.exp(high_two - highest)
    row_count, head_total = high_one.shape
    merged = (
        accum_one.reshape(row_count, head_total, -1) * factor_one[..., None]
        + accum_two.reshape(row_count, head_total, -1) * factor_two[..., None]
    )
    return (
        highest,
        total_one * factor_one + total_two * factor_two,
        merged.reshape(accum_one.shape),
    )


def body(
    query,
    cached_key_rows,
    cached_value_rows,
    row_cache_length,
    attention_output_weight,
    resid,
    feed_norm_scale,
    gate_down_weight,
    up_down_weight,
    gate_expansion_weight,
    up_expansion_weight,
    row_adapter_index,
):
    row_count = query.shape[0]
    positions = cached_key_rows.shape[1]
    group = HQ // KVH
    first_position = lax.axis_index("tp") * positions
    query_heads = query.reshape(row_count, KVH, group, HD)
    key_heads = cached_key_rows.reshape(row_count, positions, KVH, HD)
    value_heads = cached_value_rows.reshape(row_count, positions, KVH, HD)
    scores = jnp.einsum(
        "rkgd,rpkd->rkgp", query_heads, key_heads, preferred_element_type=jnp.float32
    ) * HD ** (-0.5)
    visible = (first_position + jnp.arange(positions, dtype=jnp.int32))[None, :] < row_cache_length[
        :, None
    ]
    visible = visible[:, None, None, :]
    masked = jnp.where(visible, scores, -1e30)
    highest = jnp.max(masked, axis=-1)
    weights = jnp.where(visible, jnp.exp(masked - highest[..., None]), 0.0)
    totals = jnp.sum(weights, axis=-1)
    accumulated = jnp.einsum(
        "rkgp,rpkd->rkgd",
        weights.astype(jnp.bfloat16),
        value_heads,
        preferred_element_type=jnp.float32,
    )
    highest = highest.reshape(row_count, HQ)
    totals = totals.reshape(row_count, HQ)
    accumulated = accumulated.reshape(row_count, MODEL_WIDTH)
    tensor_size = lax.axis_size("tp")
    head_count = HQ // tensor_size
    head_width = MODEL_WIDTH // tensor_size
    highest, totals, accumulated = joined((highest, totals, accumulated), "tp", combine_parts)
    own_heads = lax.dynamic_slice_in_dim(
        accumulated, lax.axis_index("tp") * head_width, head_width, 1
    )
    own_totals = lax.dynamic_slice_in_dim(totals, lax.axis_index("tp") * head_count, head_count, 1)
    attended = (
        (own_heads.reshape(row_count, head_count, HD) / own_totals[..., None])
        .reshape(row_count, head_width)
        .astype(jnp.bfloat16)
    )
    partial_value = jnp.dot(
        lax.all_gather(attended, "row", axis=0, tiled=True),
        attention_output_weight,
        preferred_element_type=jnp.float32,
    )
    projected = lax.psum_scatter(partial_value, "tp", scatter_dimension=1, tiled=True)
    hidden = resid.astype(jnp.float32) + projected
    stream = hidden.astype(jnp.bfloat16)
    squares = jnp.sum(hidden * hidden, axis=1)
    scaled_input = (hidden * feed_norm_scale.astype(jnp.float32)[None, :]).astype(jnp.bfloat16)
    batch_rows = hidden.shape[0]
    micro = lax.axis_index("grp")
    own_ids = lax.dynamic_slice_in_dim(row_adapter_index, micro * batch_rows, batch_rows)
    chosen = (own_ids[:, None] == jnp.arange(ADAPTER_COUNT, dtype=jnp.int32)[None, :]).astype(
        jnp.float32
    )

    def selected_adapter_slots(product):
        return jnp.sum(
            product.reshape(batch_rows, ADAPTER_COUNT, ADAPTER_RANK) * chosen[:, :, None], axis=1
        )

    gate_down_output = jnp.dot(scaled_input, gate_down_weight, preferred_element_type=jnp.float32)
    up_down_output = jnp.dot(scaled_input, up_down_weight, preferred_element_type=jnp.float32)
    squares, gate_down_output, up_down_output = lax.psum(
        (squares, gate_down_output, up_down_output), ("row", "tp")
    )
    gate_rank_rows = selected_adapter_slots(gate_down_output)
    up_rank_rows = selected_adapter_slots(up_down_output)
    inverse_norm = lax.rsqrt(squares / MODEL_WIDTH + epsilon)
    rank_pair = (
        jnp.concatenate([gate_rank_rows, up_rank_rows], axis=1) * inverse_norm[:, None]
    ).astype(jnp.bfloat16)
    row_group = lax.axis_index("row")
    own_pair = lax.dynamic_slice_in_dim(rank_pair, row_group * row_count, row_count, 0)
    gathered_rows = lax.all_gather(own_pair, "grp", axis=0, tiled=True)
    group_count = lax.axis_size("grp")
    adapter_rows = lax.dynamic_slice_in_dim(
        row_adapter_index.reshape(group_count, batch_rows), row_group * row_count, row_count, 1
    ).reshape(-1)
    half_adapter_slots = gate_expansion_weight.shape[0] // ADAPTER_RANK
    local_ids = adapter_rows - micro * half_adapter_slots
    owned = (local_ids[:, None] == jnp.arange(half_adapter_slots, dtype=jnp.int32)[None, :]).astype(
        jnp.float32
    )

    def expand_rows(rank_part, table):
        coefficient = (
            (owned[:, :, None] * rank_part.astype(jnp.float32)[:, None, :])
            .reshape(-1, half_adapter_slots * ADAPTER_RANK)
            .astype(jnp.bfloat16)
        )
        return jnp.dot(coefficient, table, preferred_element_type=jnp.float32)

    gate_adapter_delta = expand_rows(gathered_rows[:, :ADAPTER_RANK], gate_expansion_weight)
    up_adapter_delta = expand_rows(gathered_rows[:, ADAPTER_RANK:], up_expansion_weight)
    gate_delta, up_delta = (
        lax.psum_scatter(
            gate_adapter_delta.astype(jnp.bfloat16), "grp", scatter_dimension=0, tiled=True
        ).astype(jnp.float32),
        lax.psum_scatter(
            up_adapter_delta.astype(jnp.bfloat16), "grp", scatter_dimension=0, tiled=True
        ).astype(jnp.float32),
    )
    return (stream, gate_delta.astype(jnp.bfloat16), up_delta.astype(jnp.bfloat16))


def solution(mesh):
    return jax.shard_map(
        body,
        mesh=mesh,
        in_specs=(
            P(("grp", "row"), None),
            P(("grp", "row"), "tp", None),
            P(("grp", "row"), "tp", None),
            P(("grp", "row")),
            P("tp", "row"),
            P("grp", ("row", "tp")),
            P(("row", "tp")),
            P(("row", "tp"), None),
            P(("row", "tp"), None),
            P("grp", "tp"),
            P("grp", "tp"),
            P(),
        ),
        out_specs=(P("grp", ("row", "tp")), P(("grp", "row"), "tp"), P(("grp", "row"), "tp")),
        check_vma=False,
    )
```

profile of v0, /device:TPU:1, one launch (start us, length us, event | category | flops | bytes accessed | tf_op | source)
XLA Modules:
  0.0 1970.4 jit_solution(4430572817811749789)
XLA Ops:
  7.3 1.1 copy.25
  8.3 0.9 broadcast_compare_fusion
  9.2 0.7 fusion.33
  10.0 0.5 fusion.3
  10.4 0.9 all_gather_reshape.11
  11.4 0.3 fusion.16
  12.0 46.4 %all_gather.16 = f32[32,4,128]{2,1,0:T(4,128)S(1)} all-gather(f32[1,4,128]{2,1,0:T(4,128)S(1)} %all_gather_reshape.10), channel_id=1, replica_groups=mesh['grp'=2,'row'=4,'tp'=32] {'tp'}, dimensions={0}, use_global_device_ids=true | all-gather | bytes 67584 | tf_op jit(solution)/shard_map/all_gather | solution.py:18
  58.4 38.2 %all_gather.15 = f32[32,4,128]{2,1,0:T(4,128)S(1)} all-gather(f32[1,4,128]{2,1,0:T(4,128)S(1)} %all_gather_reshape.9), channel_id=1, replica_groups=mesh['grp'=2,'row'=4,'tp'=32] {'tp'}, dimensions={0}, use_global_device_ids=true | all-gather | bytes 67584 | tf_op jit(solution)/shard_map/all_gather | solution.py:18
  96.6 1.0 slice_bitcast_fusion
  97.6 50.3 %while.19 = (s32[]{:T(128)}, f32[4,128]{1,0:T(4,128)S(1)}, f32[4,128]{1,0:T(4,128)S(1)}, f32[4,16384]{1,0:T(4,128)S(1)}, f32[32,4,128]{2,1,0:T(4,128)S(1)}, /*in...) while((s32[]{:T(128)}, f32[4,128]{1,0:T(4,128)S(1)}, ...), condition=%wide.region_3.4_spmd, body=%wide.region_2.3_spmd.sunk | while | flops 199685 | bytes 1855639 | solution.py:23
  97.6 0.2 broadcast_bitcast_fusion.4
  97.8 1.4 fusion.53
  99.3 0.2 broadcast_bitcast_fusion.4
  99.5 1.4 fusion.53
  101.1 1.4 fusion.53
  102.7 1.4 fusion.53
  104.3 1.4 fusion.53
  105.9 1.4 fusion.53
  107.6 1.4 fusion.53
  109.2 1.4 fusion.53
  110.6 0.2 broadcast_bitcast_fusion.4
  110.8 1.4 fusion.53
  112.2 0.2 broadcast_bitcast_fusion.4
  112.4 1.4 fusion.53
  113.9 0.2 broadcast_bitcast_fusion.4
  114.1 1.4 fusion.53
  115.5 0.2 broadcast_bitcast_fusion.4
  115.7 1.4 fusion.53
  117.3 1.4 fusion.53
  118.9 1.4 fusion.53
  120.6 1.4 fusion.53
  122.2 1.4 fusion.53
  123.8 1.4 fusion.53
  125.4 1.4 fusion.53
  126.8 0.2 broadcast_bitcast_fusion.4
  127.0 1.4 fusion.53
  128.5 0.2 broadcast_bitcast_fusion.4
  128.7 1.4 fusion.53
  130.3 1.4 fusion.53
  131.9 1.4 fusion.53
  133.5 1.4 fusion.53
  135.2 1.4 fusion.53
  136.8 1.4 fusion.53
  138.4 1.4 fusion.53
  140.0 1.4 fusion.53
  141.7 1.4 fusion.53
  143.3 1.4 fusion.53
  144.9 1.4 fusion.53
  146.5 1.4 fusion.53
  148.1 9.7 all-gather
  157.9 3.6 fusion.34
  161.7 0.6 dynamic-slice
  163.1 137.4 %reduce-scatter.2.cloned.1.call-done = f32[16,128]{1,0:T(8,128)} async-done(((f32[16,4096]{1,0:T(8,128)}), f32[16,128]{1,0:T(8,128)}) %reduce-scatter.2.cloned.1.call-update) | async-done | bytes 8208 | tf_op jit(solution)/shard_map/reduce_scatter | solution.py:105
  300.5 1.4 multiply_convert_fusion.2
  302.0 1.0 reshape.157
  303.2 1.0 reshape.158
  304.2 338.3 %psum.23 = f32[16]{0:T(128)S(1)} all-reduce(f32[16]{0:T(128)S(1)} %get-tuple-element.209), channel_id=1, replica_groups=mesh['grp'=2,'row'=4,'tp'=32] {'row','tp'}, use_global_device_ids=true, to_apply=%region_10.11 | all-reduce | flops 16 | bytes 128 | tf_op jit(solution)/shard_map/psum | solution.py:124
  642.6 1294.0 %all-reduce.6.cloned.1.call-done = (f32[16,64,16]{2,1,0:T(8,128)}, f32[16,64,16]{2,1,0:T(8,128)}) async-done(((f32[16,64,16]{2,1,0:T(8,128)}, f32[16,64,16]{2,1,0:T(8,128)}), (f32[16,64,16]{2,1,0:T(8,128)}, f32[16,64,16]{2,1,0:T(8,128)})) %all-reduce.6.cloned.1.call-update) | async-done | bytes 131088 | tf_op jit(solution)/shard_map/psum | solution.py:124
  1936.7 1.4 multiply_reduce_fusion.1
  1938.2 7.0 all-gather.1
  1945.6 1.8 convolution_convert_fusion
  1947.4 1.8 convolution_convert_fusion.1
  1949.2 14.0 all-reduce.3
  1963.2 0.6 constant_dynamic-slice_fusion.2
  (102 shorter events, 7.1 us)
Async XLA Ops:
  7.2 2.1 copy-start
  7.2 89.4 %all-gather.4.cloned.1.call-start = ((), (), s32[]{:S(2)}) async-start(), calls=%async_computation.1 | async-start | bytes 8650752 | tf_op jit(solution)/shard_map/all_gather | solution.py:18
  7.2 2.7 copy-start.1
  10.0 1.8 copy-start.5
  10.0 1.8 copy-start.6
  11.3 289.2 %reduce-scatter.2.cloned.1.call-start = ((), (), s32[]{:S(2)}) async-start(), calls=%async_computation.2 | async-start | bytes 270336 | tf_op jit(solution)/shard_map/reduce_scatter | solution.py:105
  157.8 3.9 copy-start.7
  157.8 142.7 %copy-start.4 = (bf16[16,128]{1,0:T(8,128)(2,1)S(1)}, bf16[16,128]{1,0:T(8,128)(2,1)}, u32[]{:S(2)}) copy-start(bf16[16,128]{1,0:T(8,128)(2,1)} %param.19) | copy-start | bytes 12292
  157.8 144.0 %copy-start.2 = (bf16[128,1024]{1,0:T(8,128)(2,1)S(1)}, bf16[128,1024]{1,0:T(8,128)(2,1)}, u32[]{:S(2)}) copy-start(bf16[128,1024]{1,0:T(8,128)(2,1)} %param.21) | copy-start | bytes 786436
  157.8 145.2 %copy-start.3 = (bf16[128,1024]{1,0:T(8,128)(2,1)S(1)}, bf16[128,1024]{1,0:T(8,128)(2,1)}, u32[]{:S(2)}) copy-start(bf16[128,1024]{1,0:T(8,128)(2,1)} %param.22) | copy-start | bytes 786436
  161.5 1775.2 %all-reduce.6.cloned.1.call-start = ((), (), s32[]{:S(2)}) async-start(), calls=%async_computation.3 | async-start | bytes 2097152 | tf_op jit(solution)/shard_map/psum | solution.py:124
Sparse Core Ops, SparseCore 0:
  11.4 73.3 all-gather.3
  161.6 138.8 reduce-scatter.1
  642.7 1293.9 all-reduce.5
where the time goes:
time: 1980 us; the launch traced here: 1970 us
  waiting for transfers between devices  1430 us (72%)
  blocking collectives  454 us (23%)
  other arithmetic  48.2 us (2%)
    psum x1, waiting for transfers between devices, body(): lax.psum((squares, gate_down_output, up_down_output), ('row', 'tp'))  1290 us
    psum x1, blocking collectives, body(): lax.psum((squares, gate_down_output, up_down_output), ('row', 'tp'))  338 us
    reduce_scatter x1, waiting for transfers between devices, body(): lax.psum_scatter(partial_value, 'tp', scatter_dimension=1, tiled=True)  137 us
    all_gather x2, blocking collectives, joined(): gathered = jax.tree.map(lambda a: lax.all_gather(a, axis), part)  84.6 us
    add x31, other arithmetic, combine_parts(): accum_one.reshape(row_count, head_total, -1) * factor_one[..., None]  42.9 us
  transfers between devices with their start and end apart: 3, of which 2 were waited for; matrix products, arithmetic and copies ran while one was open for 0% of the time, Pallas kernels for 0%

commit v1 on v0

v1 whole, which is shorter than its diff:
```python
import functools

import jax
import jax.numpy as jnp
from jax import lax
from jax.experimental import pallas as pl
from jax.experimental.pallas import tpu as pltpu
from jax.sharding import PartitionSpec as P

HD = 128
RANK = 16
EPSILON = 1e-05
MESH = pl.DeviceIdType.MESH
F32 = jnp.float32
BF16 = jnp.bfloat16


def iota(shape, axis):
    return lax.broadcasted_iota(jnp.int32, shape, axis)


def kernel(
    sizes,
    lengths,
    ids,
    query_hbm,
    key_hbm,
    value_hbm,
    wo_hbm,
    resid_hbm,
    gain_hbm,
    gate_down_hbm,
    up_down_hbm,
    gate_exp_hbm,
    up_exp_hbm,
    stream_out,
    gate_out,
    up_out,
    query,
    keys,
    values,
    wo,
    resid,
    gain,
    down,
    expand,
    acc_s,
    stat_s,
    msg_s,
    send_b,
    send_st,
    recv_b,
    recv_st,
    recv_c,
    send_d,
    recv_d,
    send_e,
    recv_e,
    recv_g,
    send_f,
    recv_f,
    load_sem,
    kv_sem,
    send_sem,
    recv_sem,
):
    n_grp, n_row, n_tp = sizes
    rows, positions, kv_width = keys.shape
    kv_heads = kv_width // HD
    heads = query.shape[1] // HD
    group = heads // kv_heads
    per = heads // n_tp
    tile = rows * per
    micro_rows = n_row * rows
    grp = lax.axis_index("grp")
    row = lax.axis_index("row")
    me = lax.axis_index("tp")

    def load(source, target, index):
        copy = pltpu.make_async_copy(source, target, load_sem.at[index])
        copy.start()
        return copy

    def wait_bytes(ref, sem):
        pltpu.make_async_copy(ref, ref, sem).wait()

    query_copy = load(query_hbm, query, 0)
    kv_copies = []
    for b in range(rows):
        pair = (
            pltpu.make_async_copy(key_hbm.at[b], keys.at[b], kv_sem.at[0, b]),
            pltpu.make_async_copy(value_hbm.at[b], values.at[b], kv_sem.at[1, b]),
        )
        for copy in pair:
            copy.start()
        kv_copies.append(pair)
    wo_copy = load(wo_hbm, wo, 1)
    resid_copy = load(resid_hbm, resid, 2)
    gain_copy = load(gain_hbm, gain, 3)
    down_copies = (load(gate_down_hbm, down.at[0], 4), load(up_down_hbm, down.at[1], 5))
    expand_copies = (load(gate_exp_hbm, expand.at[0], 6), load(up_exp_hbm, expand.at[1], 7))

    barrier = pltpu.get_barrier_semaphore()
    for k in range(1, n_row):
        pl.semaphore_signal(
            barrier, inc=1, device_id={"row": lax.rem(row + k, n_row)}, device_id_type=MESH
        )

    def greet(k, carry):
        there = lax.rem(me + k, n_tp)

        @pl.when(k > 0)
        def _():
            pl.semaphore_signal(barrier, inc=1, device_id={"tp": there}, device_id_type=MESH)

        pl.semaphore_signal(
            barrier, inc=1, device_id={"grp": 1 - grp, "tp": there}, device_id_type=MESH
        )
        return carry

    lax.fori_loop(0, n_tp, greet, 0)

    query_copy.wait()
    head_rows = query[...].astype(F32).reshape(rows, heads, HD).astype(BF16)
    position = me * positions + iota((heads, positions), 1)
    stat_lane = iota((heads, HD), 1) - rows * lax.rem(iota((heads, HD), 0), per)
    stats = jnp.zeros((heads, HD), F32)
    for b in range(rows):
        for copy in kv_copies[b]:
            copy.wait()
        scores = jnp.concatenate(
            [
                lax.dot_general(
                    head_rows[b, k * group : (k + 1) * group],
                    keys[b, :, k * HD : (k + 1) * HD],
                    (((1,), (1,)), ((), ())),
                    preferred_element_type=F32,
                )
                for k in range(kv_heads)
            ],
            axis=0,
        ) * (HD ** (-0.5))
        visible = position < lengths[b]
        masked = jnp.where(visible, scores, -1e30)
        highest = jnp.max(masked, axis=1, keepdims=True)
        weights = jnp.where(visible, jnp.exp(masked - highest), 0.0)
        total = jnp.sum(weights, axis=1, keepdims=True)
        weights = weights.astype(BF16)
        for k in range(kv_heads):
            acc_s[b, k * group : (k + 1) * group, :] = jnp.dot(
                weights[k * group : (k + 1) * group],
                values[b, :, k * HD : (k + 1) * HD],
                preferred_element_type=F32,
            )
        stats = jnp.where(stat_lane == b, highest, stats)
        stats = jnp.where(stat_lane == tile + b, total, stats)
        for j in range(per):
            msg_s[pl.ds(j * rows + b, n_tp, stride=tile), :] = acc_s[
                b, pl.ds(j, n_tp, stride=per), :
            ]
    send_b[...] = msg_s[...].reshape(n_tp, tile, HD).astype(BF16)
    stat_s[...] = stats
    stat_rows = stat_s[pl.ds(0, n_tp, stride=per), :]
    for j in range(1, per):
        stat_rows += stat_s[pl.ds(j, n_tp, stride=per), :]
    send_st[...] = stat_rows.reshape(n_tp, 1, HD)

    pl.semaphore_wait(barrier, n_row - 1 + 2 * n_tp - 1)

    def remote(source, target, index, device):
        return pltpu.make_async_remote_copy(
            src_ref=source,
            dst_ref=target,
            send_sem=send_sem.at[index],
            recv_sem=recv_sem.at[index],
            device_id=device,
            device_id_type=MESH,
        )

    def send_partial(k, carry):
        there = lax.rem(me + k, n_tp)
        remote(send_st.at[there], recv_st.at[k - 1], 1, {"tp": there}).start()
        remote(send_b.at[there], recv_b.at[k - 1], 0, {"tp": there}).start()
        return carry

    lax.fori_loop(1, n_tp, send_partial, 0)
    recv_b[n_tp - 1] = send_b[me]
    recv_st[n_tp - 1] = send_st[me]
    wait_bytes(recv_st.at[0 : n_tp - 1], recv_sem.at[1])

    part_stats = recv_st[...].reshape(n_tp, HD)
    overall = jnp.max(part_stats, axis=0, keepdims=True)
    factor = jnp.exp(part_stats - overall)
    part_totals = pltpu.roll(part_stats, HD - tile, 1)
    normal = jnp.sum(factor * part_totals, axis=0, keepdims=True)
    share = jnp.where(iota((n_tp, HD), 1) < tile, factor / normal, 0.0)
    share = share.T[:tile]
    wait_bytes(recv_b.at[0 : n_tp - 1], recv_sem.at[0])
    attended = jnp.zeros((tile, HD), F32)
    for s in range(n_tp):
        attended += share[:, s : s + 1] * recv_b[s].astype(F32)

    recv_c[row] = attended.astype(BF16)
    for k in range(1, n_row):
        remote(recv_c.at[row], recv_c.at[row], 2, {"row": lax.rem(row + k, n_row)}).start()
    wait_bytes(recv_c.at[0 : n_row - 1], recv_sem.at[2])
    gathered = recv_c[...].astype(F32)
    left = jnp.concatenate(
        [
            jnp.concatenate(
                [gathered[r, j * rows : (j + 1) * rows] for r in range(n_row)], axis=0
            )
            for j in range(per)
        ],
        axis=1,
    ).astype(BF16)

    wo_copy.wait()

    def project(k, carry):
        pair = lax.rem(lax.div(me, 2) + k, n_tp // 2)
        columns = pl.ds(pl.multiple_of(pair * 2 * HD, 2 * HD), 2 * HD)
        product = jnp.dot(left, wo[:, columns], preferred_element_type=F32).astype(BF16)
        for half in range(2):
            there = pair * 2 + half
            send_d[there] = product[:, half * HD : (half + 1) * HD]
            distance = lax.rem(there - me + n_tp, n_tp)

            @pl.when(distance > 0)
            def _():
                remote(send_d.at[there], recv_d.at[distance - 1], 3, {"tp": there}).start()

        return carry

    lax.fori_loop(1, n_tp // 2 + 1, project, 0)
    recv_d[n_tp - 1] = send_d[me]

    def id_column(base, count, shape, start, column):
        for i in range(count):
            column = jnp.where(iota(shape, 0) == start + i, ids[base + i], column)
        return column

    micro_ids = id_column(
        grp * micro_rows, micro_rows, (micro_rows, HD), 0, jnp.zeros((micro_rows, HD), jnp.int32)
    )
    lane_adapter = lax.div(iota((micro_rows, HD), 1), RANK)
    resid_copy.wait()
    gain_copy.wait()
    for copy in down_copies:
        copy.wait()
    wait_bytes(recv_d.at[0 : n_tp - 1], recv_sem.at[3])
    hidden = resid[...].astype(F32)
    projected = recv_d[0].astype(F32)
    for s in range(1, n_tp):
        projected += recv_d[s].astype(F32)
    hidden = hidden + projected
    stream_out[...] = hidden.astype(BF16)
    squares = jnp.sum(hidden * hidden, axis=1, keepdims=True)
    scaled = (hidden * gain[...].astype(F32).reshape(1, HD)).astype(BF16)

    def selected(table):
        product = jnp.dot(scaled, table, preferred_element_type=F32)
        per_chunk = HD // RANK
        chosen = jnp.zeros((micro_rows, HD), F32)
        for c in range(product.shape[1] // HD):
            chosen += jnp.where(
                lane_adapter + c * per_chunk == micro_ids, product[:, c * HD : (c + 1) * HD], 0.0
            )
        shift = HD // 2
        while shift >= RANK:
            chosen += pltpu.roll(chosen, shift, 1)
            shift //= 2
        return chosen

    lane = iota((micro_rows, HD), 1)
    part = jnp.where(
        lane < RANK,
        selected(down[0]),
        jnp.where(
            lane < 2 * RANK, selected(down[1]), jnp.where(lane == 2 * RANK, squares, 0.0)
        ),
    )

    for r in range(n_row):
        send_e[r] = part[r * rows : (r + 1) * rows]
    for k in range(1, n_row):
        there = lax.rem(row + k, n_row)
        remote(send_e.at[there], recv_e.at[k - 1], 4, {"row": there}).start()
    recv_e[n_row - 1] = send_e[row]
    wait_bytes(recv_e.at[0 : n_row - 1], recv_sem.at[4])
    summed = recv_e[0]
    for s in range(1, n_row):
        summed += recv_e[s]

    recv_g[n_tp - 1] = summed

    def spread(k, carry):
        there = lax.rem(me + k, n_tp)

        @pl.when(k > 0)
        def _():
            remote(recv_g.at[n_tp - 1], recv_g.at[k - 1], 5, {"tp": there}).start()

        remote(
            recv_g.at[n_tp - 1], recv_g.at[n_tp + k], 6, {"grp": 1 - grp, "tp": there}
        ).start()
        return carry

    lax.fori_loop(0, n_tp, spread, 0)
    both = 2 * rows
    pair_ids = id_column(
        grp * micro_rows + row * rows, rows, (both, HD), 0, jnp.zeros((both, HD), jnp.int32)
    )
    pair_ids = id_column(
        (1 - grp) * micro_rows + row * rows, rows, (both, HD), rows, pair_ids
    )
    half_adapters = expand.shape[1] // RANK
    local_ids = pair_ids - grp * half_adapters
    pair_adapter = lax.div(iota((both, HD), 1), RANK)
    for copy in expand_copies:
        copy.wait()
    wait_bytes(recv_g.at[0 : n_tp - 1], recv_sem.at[5])
    wait_bytes(recv_g.at[n_tp : 2 * n_tp], recv_sem.at[6])
    sums = []
    for half in range(2):
        sum_half = recv_g[half * n_tp]
        for s in range(1, n_tp):
            sum_half += recv_g[half * n_tp + s]
        sums.append(sum_half)
    sums = jnp.concatenate(sums, axis=0)
    inverse = lax.rsqrt(sums[:, 2 * RANK : 2 * RANK + 1] / (n_row * n_tp * HD) + EPSILON)
    ranks = (sums * inverse).astype(BF16).astype(F32)
    pair_lane = iota((both, HD), 1)

    deltas = []
    for which in range(2):
        spread_rank = ranks if which == 0 else pltpu.roll(ranks, HD - RANK, 1)
        spread_rank = jnp.where(pair_lane < RANK, spread_rank, 0.0)
        shift = RANK
        while shift < HD:
            spread_rank += pltpu.roll(spread_rank, shift, 1)
            shift *= 2
        per_chunk = HD // RANK
        coefficient = jnp.concatenate(
            [
                jnp.where(pair_adapter + c * per_chunk == local_ids, spread_rank, 0.0)
                for c in range(half_adapters // per_chunk)
            ],
            axis=1,
        ).astype(BF16)
        deltas.append(jnp.dot(coefficient, expand[which], preferred_element_type=F32))

    chunks = deltas[0].shape[1] // HD
    stack = recv_f.shape[1] // rows
    pieces = [
        deltas[which][rows:, c * HD : (c + 1) * HD] for which in range(2) for c in range(chunks)
    ]
    pieces += [jnp.zeros((rows, HD), F32)] * (-len(pieces) % stack)
    for i in range(len(pieces) // stack):
        send_f[i] = jnp.concatenate(pieces[i * stack : (i + 1) * stack], axis=0).astype(BF16)
    remote(send_f, recv_f, 7, {"grp": 1 - grp}).start()
    wait_bytes(recv_f, recv_sem.at[7])
    outs = (gate_out, up_out)
    for which in range(2):
        for c in range(chunks):
            at = which * chunks + c
            other = recv_f[at // stack].astype(F32)[at % stack * rows : (at % stack + 1) * rows]
            own = deltas[which][:rows, c * HD : (c + 1) * HD].astype(BF16).astype(F32)
            outs[which][:, c * HD : (c + 1) * HD] = (own + other).astype(BF16)

    wait_bytes(recv_b.at[0 : n_tp - 1], send_sem.at[0])
    wait_bytes(recv_st.at[0 : n_tp - 1], send_sem.at[1])
    wait_bytes(recv_c.at[0 : n_row - 1], send_sem.at[2])
    wait_bytes(recv_d.at[0 : n_tp - 1], send_sem.at[3])
    wait_bytes(recv_e.at[0 : n_row - 1], send_sem.at[4])
    wait_bytes(recv_g.at[0 : n_tp - 1], send_sem.at[5])
    wait_bytes(recv_g.at[n_tp : 2 * n_tp], send_sem.at[6])
    wait_bytes(send_f, send_sem.at[7])


def layer(
    sizes,
    query,
    cached_key_rows,
    cached_value_rows,
    row_cache_length,
    attention_output_weight,
    resid,
    feed_norm_scale,
    gate_down_weight,
    up_down_weight,
    gate_expansion_weight,
    up_expansion_weight,
    row_adapter_index,
):
    n_grp, n_row, n_tp = sizes
    rows = query.shape[0]
    heads = query.shape[1] // HD
    tile = rows * (heads // n_tp)
    columns = gate_expansion_weight.shape[1]
    stack = 16 // rows
    packed = -(-2 * (columns // HD) // stack)
    smem = pl.BlockSpec(memory_space=pltpu.SMEM)
    hbm = pl.BlockSpec(memory_space=pl.ANY)
    vmem = pl.BlockSpec(memory_space=pltpu.VMEM)
    return pl.pallas_call(
        functools.partial(kernel, sizes),
        out_shape=(
            jax.ShapeDtypeStruct(resid.shape, BF16),
            jax.ShapeDtypeStruct((rows, columns), BF16),
            jax.ShapeDtypeStruct((rows, columns), BF16),
        ),
        in_specs=[smem] * 2 + [hbm] * 10,
        out_specs=(vmem,) * 3,
        scratch_shapes=[
            pltpu.VMEM(query.shape, BF16),
            pltpu.VMEM(cached_key_rows.shape, BF16),
            pltpu.VMEM(cached_value_rows.shape, BF16),
            pltpu.VMEM(attention_output_weight.shape, BF16),
            pltpu.VMEM(resid.shape, BF16),
            pltpu.VMEM(feed_norm_scale.shape, BF16),
            pltpu.VMEM((2,) + gate_down_weight.shape, BF16),
            pltpu.VMEM((2,) + gate_expansion_weight.shape, BF16),
            pltpu.VMEM((rows, heads, HD), F32),
            pltpu.VMEM((heads, HD), F32),
            pltpu.VMEM((n_tp * tile, HD), F32),
            pltpu.VMEM((n_tp, tile, HD), BF16),
            pltpu.VMEM((n_tp, 1, HD), F32),
            pltpu.VMEM((n_tp, tile, HD), BF16),
            pltpu.VMEM((n_tp, 1, HD), F32),
            pltpu.VMEM((n_row, tile, HD), BF16),
            pltpu.VMEM((n_tp, n_row * rows, HD), BF16),
            pltpu.VMEM((n_tp, n_row * rows, HD), BF16),
            pltpu.VMEM((n_row, rows, HD), F32),
            pltpu.VMEM((n_row, rows, HD), F32),
            pltpu.VMEM((2 * n_tp, rows, HD), F32),
            pltpu.VMEM((packed, 16, HD), BF16),
            pltpu.VMEM((packed, 16, HD), BF16),
            pltpu.SemaphoreType.DMA((8,)),
            pltpu.SemaphoreType.DMA((2, rows)),
            pltpu.SemaphoreType.DMA((8,)),
            pltpu.SemaphoreType.DMA((8,)),
        ],
        compiler_params=pltpu.CompilerParams(
            collective_id=0, has_side_effects=True, vmem_limit_bytes=56 * 1024 * 1024
        ),
    )(
        row_cache_length,
        row_adapter_index,
        query,
        cached_key_rows,
        cached_value_rows,
        attention_output_weight,
        resid,
        feed_norm_scale,
        gate_down_weight,
        up_down_weight,
        gate_expansion_weight,
        up_expansion_weight,
    )


def solution(mesh):
    sizes = tuple(mesh.shape[axis] for axis in ("grp", "row", "tp"))
    return jax.shard_map(
        functools.partial(layer, sizes),
        mesh=mesh,
        in_specs=(
            P(("grp", "row"), None),
            P(("grp", "row"), "tp", None),
            P(("grp", "row"), "tp", None),
            P(("grp", "row")),
            P("tp", "row"),
            P("grp", ("row", "tp")),
            P(("row", "tp")),
            P(("row", "tp"), None),
            P(("row", "tp"), None),
            P("grp", "tp"),
            P("grp", "tp"),
            P(),
        ),
        out_specs=(P("grp", ("row", "tp")), P(("grp", "row"), "tp"), P(("grp", "row"), "tp")),
        check_vma=False,
    )
```

time: 1980 us -> 49.8 us (0.03)
  waiting for transfers between devices: 1430 us -> 0 us
  blocking collectives: 454 us -> 0 us
  other arithmetic: 48.2 us -> 0 us
  Pallas kernels: 0 us -> 44.9 us
    psum x1 -> x0, waiting for transfers between devices: 1290 us -> none  [body(): lax.psum((squares, gate_down_output, up_down_output), ('row', 'tp'))]
    psum x1 -> x0, blocking collectives: 338 us -> none  [body(): lax.psum((squares, gate_down_output, up_down_output), ('row', 'tp'))]
    reduce_scatter x1 -> x0, waiting for transfers between devices: 137 us -> none  [body(): lax.psum_scatter(partial_value, 'tp', scatter_dimension=1, tiled=True)]
    all_gather x4 -> x0, blocking collectives: 101 us -> none  [the longest x2 84.6 us: joined(): gathered = jax.tree.map(lambda a: lax.all_gather(a, axis), part)]
    pallas_call x0 -> x1, Pallas kernels: none -> 44.9 us  [layer(): pl.pallas_call(functools.partial(kernel, sizes), out_shape=(jax.ShapeDtyp...]
    add x63 -> x0, other arithmetic: 43.7 us -> none  [the longest x31 42.9 us: combine_parts(): accum_one.reshape(row_count, head_total, -1) * factor_one[..., None]]
  transfers between devices with their start and end apart: 3 -> 0, of which waited for: 2 -> 0; matrix products, arithmetic and copies ran while one was open for 0% -> 0% of each run, Pallas kernels for 0% -> 0%
where the time goes in v1:
time: 49.8 us; the launch traced here: 49.4 us
  Pallas kernels  44.9 us (90%)
  local copies, waits for them, and re-layouts  3.9 us (8%)
  between operations  0.64 us (1%)
    pallas_call x1, Pallas kernels, layer(): pl.pallas_call(functools.partial(kernel, sizes), out_shape=(jax.ShapeDtyp...  44.9 us
    unnamed x3, local copies, waits for them, and re-layouts  3.9 us

profile of v1, /device:TPU:1, one launch (start us, length us, event | category | flops | bytes accessed | tf_op | source)
XLA Modules:
  0.0 49.4 jit_solution(3162214356556385654)
XLA Ops:
  0.6 44.9 %shard_map.139 = (bf16[16,128]{1,0:T(8,128)(2,1)}, bf16[4,1664]{1,0:T(4,128)(2,1)}, bf16[4,1664]{1,0:T(4,128)(2,1)}) custom-call(s32[4]{0:T(128)} %lengths.1, s32[32]{0:T(128)} %ids.1, bf16[4,16384]{1,0:T(4,128)(2,1)} %query_hbm.1, bf16[4,256,1024]{2,1,0:T(8,128)(2,1)} %key_hbm.1, bf16[4,256,1024]{2,1,0:T(8,128)(2,1)} %value_hbm.1, ...), custom_call_target="tpu_custom_call" | custom-call | tf_op jit(solution)/shard_map/pallas_call | solution.py:406
  45.5 1.3 %copy.18 = bf16[16,128]{1,0:T(8,128)(2,1)} copy(bf16[16,128]{1,0:T(8,128)(2,1)} %get-tuple-element.6) | data formatting | bytes 8192
  46.8 1.3 %copy.19 = bf16[4,1664]{1,0:T(4,128)(2,1)} copy(bf16[4,1664]{1,0:T(4,128)(2,1)} %get-tuple-element.7) | data formatting | bytes 26624
  48.1 1.3 %copy.20 = bf16[4,1664]{1,0:T(4,128)(2,1)} copy(bf16[4,1664]{1,0:T(4,128)(2,1)} %get-tuple-element.8) | data formatting | bytes 26624

commit v2 on v1

v2 whole, which is shorter than its diff:
```python
import functools

import jax
import jax.numpy as jnp
from jax import lax
from jax.experimental import pallas as pl
from jax.experimental.pallas import tpu as pltpu
from jax.sharding import PartitionSpec as P

HD = 128
RANK = 16
EPSILON = 1e-05
MESH = pl.DeviceIdType.MESH
F32 = jnp.float32
BF16 = jnp.bfloat16


def iota(shape, axis):
    return lax.broadcasted_iota(jnp.int32, shape, axis)


def kernel(
    sizes,
    lengths,
    ids,
    query_hbm,
    key_hbm,
    value_hbm,
    wo_hbm,
    resid_hbm,
    gain_hbm,
    gate_down_hbm,
    up_down_hbm,
    gate_exp_hbm,
    up_exp_hbm,
    stream_out,
    gate_out,
    up_out,
    query,
    keys,
    values,
    wo,
    resid,
    gain,
    down,
    expand,
    weights_s,
    acc_s,
    share_s,
    stat_s,
    msg_s,
    send_b,
    send_st,
    recv_b,
    recv_st,
    recv_c,
    send_d,
    recv_d,
    send_e,
    recv_e,
    recv_g,
    send_f,
    recv_f,
    chosen_rows,
    load_sem,
    kv_sem,
    send_sem,
    recv_sem,
):
    n_grp, n_row, n_tp = sizes
    rows, positions, kv_width = keys.shape
    kv_heads = kv_width // HD
    heads = query.shape[1] // HD
    group = heads // kv_heads
    per = heads // n_tp
    tile = rows * per
    micro_rows = n_row * rows
    grp = lax.axis_index("grp")
    row = lax.axis_index("row")
    me = lax.axis_index("tp")

    def load(source, target, index):
        copy = pltpu.make_async_copy(source, target, load_sem.at[index])
        copy.start()
        return copy

    def wait_bytes(ref, sem):
        pltpu.make_async_copy(ref, ref, sem).wait()

    quarter = n_tp // 4
    plane = lax.div(me, quarter)
    place = lax.rem(me, quarter)
    n_core = min(2, quarter)
    n_x = quarter // n_core
    place_x = lax.div(place, n_core)
    core = lax.rem(place, n_core)
    n_near = 4 * n_core

    def other_plane(turn):
        high = lax.rem(lax.div(plane, 2) + turn // 2, 2)
        return 2 * high + lax.rem(plane + turn % 2, 2)

    def ahead(there):
        return lax.rem(there - me + n_tp, n_tp)

    query_copy = load(query_hbm, query, 0)
    key_copies = [
        pltpu.make_async_copy(key_hbm.at[b], keys.at[b], kv_sem.at[0, b]) for b in range(rows)
    ]
    value_copies = [
        pltpu.make_async_copy(value_hbm.at[b], values.at[b], kv_sem.at[1, b]) for b in range(rows)
    ]
    for copy in key_copies + value_copies:
        copy.start()

    barrier = pltpu.get_barrier_semaphore()

    def same_plane(dx):
        return plane * quarter + lax.rem(place_x + dx, n_x) * n_core + core

    def same_column(i):
        there = lax.rem(plane + i // n_core, 4) * quarter + place_x * n_core
        return there + lax.rem(core + i % n_core, n_core)

    def greet(k, carry):
        there = lax.rem(me + k, n_tp)
        pl.semaphore_signal(barrier, inc=1, device_id={"tp": there}, device_id_type=MESH)
        return carry

    for i in range(n_near):
        pl.semaphore_signal(
            barrier,
            inc=1,
            device_id={"grp": 1 - grp, "tp": same_column(i)},
            device_id_type=MESH,
        )
    lax.fori_loop(1, n_tp, greet, 0)
    for dr in range(1, n_row):
        for dx in range(n_x):
            pl.semaphore_signal(
                barrier,
                inc=1,
                device_id={"row": lax.rem(row + dr, n_row), "tp": same_plane(dx)},
                device_id_type=MESH,
            )

    query_copy.wait()
    head_rows = query[...].astype(F32).reshape(rows, heads, HD).astype(BF16)
    position = me * positions + iota((heads, positions), 1)
    stat_lane = iota((heads, HD), 1) - rows * lax.rem(iota((heads, HD), 0), per)
    stats = jnp.zeros((heads, HD), F32)
    for b in range(rows):
        key_copies[b].wait()
        scores = jnp.concatenate(
            [
                lax.dot_general(
                    head_rows[b, k * group : (k + 1) * group],
                    keys[b, :, k * HD : (k + 1) * HD],
                    (((1,), (1,)), ((), ())),
                    preferred_element_type=F32,
                )
                for k in range(kv_heads)
            ],
            axis=0,
        ) * (HD ** (-0.5))
        visible = position < lengths[b]
        masked = jnp.where(visible, scores, -1e30)
        highest = jnp.max(masked, axis=1, keepdims=True)
        weights = jnp.where(visible, jnp.exp(masked - highest), 0.0)
        total = jnp.sum(weights, axis=1, keepdims=True)
        weights_s[b] = weights.astype(BF16)
        stats = jnp.where(stat_lane == b, highest, stats)
        stats = jnp.where(stat_lane == tile + b, total, stats)
    stat_s[...] = stats
    stat_rows = stat_s[pl.ds(0, n_tp, stride=per), :]
    for j in range(1, per):
        stat_rows += stat_s[pl.ds(j, n_tp, stride=per), :]
    send_st[...] = stat_rows.reshape(n_tp, 1, HD)

    pl.semaphore_wait(barrier, n_tp - 1 + (n_row - 1) * n_x + n_near)

    def remote(source, target, index, device):
        return pltpu.make_async_remote_copy(
            src_ref=source,
            dst_ref=target,
            send_sem=send_sem.at[index],
            recv_sem=recv_sem.at[index],
            device_id=device,
            device_id_type=MESH,
        )

    def send_stats(k, carry):
        there = lax.rem(me + k, n_tp)
        remote(send_st.at[there], recv_st.at[k - 1], 1, {"tp": there}).start()
        return carry

    lax.fori_loop(1, n_tp, send_stats, 0)
    recv_st[n_tp - 1] = send_st[me]
    wo_copy = load(wo_hbm, wo, 1)
    resid_copy = load(resid_hbm, resid, 2)
    gain_copy = load(gain_hbm, gain, 3)
    down_copies = (load(gate_down_hbm, down.at[0], 4), load(up_down_hbm, down.at[1], 5))
    expand_copies = (load(gate_exp_hbm, expand.at[0], 6), load(up_exp_hbm, expand.at[1], 7))

    for b in range(rows):
        value_copies[b].wait()
        weights = weights_s[b]
        for k in range(kv_heads):
            acc_s[b, k * group : (k + 1) * group, :] = jnp.dot(
                weights[k * group : (k + 1) * group],
                values[b, :, k * HD : (k + 1) * HD],
                preferred_element_type=F32,
            )
        for j in range(per):
            msg_s[pl.ds(j * rows + b, n_tp, stride=tile), :] = acc_s[
                b, pl.ds(j, n_tp, stride=per), :
            ]
    send_b[...] = msg_s[...].reshape(n_tp, tile, HD).astype(BF16)

    def send_partial(k, carry):
        there = lax.rem(me + k, n_tp)
        remote(send_b.at[there], recv_b.at[k - 1], 0, {"tp": there}).start()
        return carry

    lax.fori_loop(1, n_tp, send_partial, 0)
    recv_b[n_tp - 1] = send_b[me]

    wait_bytes(recv_st.at[0 : n_tp - 1], recv_sem.at[1])
    part_stats = recv_st[...].reshape(n_tp, HD)
    overall = jnp.max(part_stats, axis=0, keepdims=True)
    factor = jnp.exp(part_stats - overall)
    part_totals = pltpu.roll(part_stats, HD - tile, 1)
    normal = jnp.sum(factor * part_totals, axis=0, keepdims=True)
    share = jnp.where(iota((n_tp, HD), 1) < tile, factor / normal, 0.0)
    share = share.T[:tile]
    for s in range(n_tp):
        share_s[s] = jnp.broadcast_to(share[:, s : s + 1], (tile, HD))
    wait_bytes(recv_b.at[0 : n_tp - 1], recv_sem.at[0])
    attended = share_s[0] * recv_b[0].astype(F32)
    for s in range(1, n_tp):
        attended += share_s[s] * recv_b[s].astype(F32)

    recv_c[row] = attended.astype(BF16)
    for k in range(1, n_row):
        remote(recv_c.at[row], recv_c.at[row], 2, {"row": lax.rem(row + k, n_row)}).start()
    wait_bytes(recv_c.at[0 : n_row - 1], recv_sem.at[2])
    gathered = recv_c[...].astype(F32)
    left = jnp.concatenate(
        [
            jnp.concatenate(
                [gathered[r, j * rows : (j + 1) * rows] for r in range(n_row)], axis=0
            )
            for j in range(per)
        ],
        axis=1,
    ).astype(BF16)

    wo_copy.wait()
    for turn in (3, 2, 1, 0):
        first = other_plane(turn) * quarter
        columns = pl.ds(pl.multiple_of(first * HD, quarter * HD), quarter * HD)
        product = jnp.dot(left, wo[:, columns], preferred_element_type=F32).astype(BF16)
        for i in range(quarter):
            send_d[first + i] = product[:, i * HD : (i + 1) * HD]

        def send_sums(i, carry, first=first):
            there = first + lax.rem(place + i, quarter)
            remote(send_d.at[there], recv_d.at[ahead(there) - 1], 3, {"tp": there}).start()
            return carry

        lax.fori_loop(0 if turn else 1, quarter, send_sums, 0)

    recv_d[n_tp - 1] = send_d[me]

    def id_column(base, count, shape, start, column):
        for i in range(count):
            column = jnp.where(iota(shape, 0) == start + i, ids[base + i], column)
        return column

    micro_ids = id_column(
        grp * micro_rows, micro_rows, (micro_rows, HD), 0, jnp.zeros((micro_rows, HD), jnp.int32)
    )
    lane_adapter = lax.div(iota((micro_rows, HD), 1), RANK)
    half_adapters = expand.shape[1] // RANK
    picked = rows * RANK
    group_row = iota((rows, HD), 0)
    group_lane = iota((rows, HD), 1)
    chunks = expand.shape[2] // HD
    stack = recv_f.shape[1] // rows
    tiles = recv_f.shape[0]
    early = chunks // stack
    keep = lax.div(group_lane, RANK) == group_row
    wanted = jnp.zeros((2 * picked, HD), jnp.int32)
    pick_row = iota((2 * picked, HD), 0)
    for half in range(2):
        of_grp = 1 - grp if half == 0 else grp
        for i in range(rows):
            wanted = jnp.where(
                lax.div(pick_row, RANK) == half * rows + i,
                ids[of_grp * micro_rows + row * rows + i],
                wanted,
            )
    wanted = (wanted - grp * half_adapters) * RANK + lax.rem(pick_row, RANK)
    pick_lane = iota((2 * picked, HD), 1)
    pick = jnp.concatenate(
        [
            jnp.where(pick_lane + c * HD == wanted, 1.0, 0.0)
            for c in range(half_adapters * RANK // HD)
        ],
        axis=1,
    ).astype(BF16)
    for copy in expand_copies:
        copy.wait()
    for which in range(2):
        chosen_rows[which] = jnp.dot(
            pick, expand[which], preferred_element_type=F32
        ).astype(BF16)

    resid_copy.wait()
    gain_copy.wait()
    for copy in down_copies:
        copy.wait()
    wait_bytes(recv_d.at[0 : n_tp - 1], recv_sem.at[3])
    hidden = resid[...].astype(F32)
    projected = recv_d[0].astype(F32)
    for s in range(1, n_tp):
        projected += recv_d[s].astype(F32)
    hidden = hidden + projected
    stream_out[...] = hidden.astype(BF16)
    squares = jnp.sum(hidden * hidden, axis=1, keepdims=True)
    scaled = (hidden * gain[...].astype(F32).reshape(1, HD)).astype(BF16)

    def selected(table):
        product = jnp.dot(scaled, table, preferred_element_type=F32)
        per_chunk = HD // RANK
        chosen = jnp.zeros((micro_rows, HD), F32)
        for c in range(product.shape[1] // HD):
            chosen += jnp.where(
                lane_adapter + c * per_chunk == micro_ids, product[:, c * HD : (c + 1) * HD], 0.0
            )
        shift = HD // 2
        while shift >= RANK:
            chosen += pltpu.roll(chosen, shift, 1)
            shift //= 2
        return chosen

    lane = iota((micro_rows, HD), 1)
    own_row = lax.rem(iota((micro_rows, HD), 0), rows)
    ranks = jnp.where(
        lax.rem(lax.div(lane, RANK), 2) == 0, selected(down[0]), selected(down[1])
    )
    ranks = jnp.where(lax.div(lane, 2 * RANK) == own_row, ranks, 0.0)
    squares = jnp.where(lane == own_row, squares, 0.0)

    for r in range(n_row):
        of_group = slice(r * rows, (r + 1) * rows)
        send_e[r, 0:1] = jnp.sum(ranks[of_group], axis=0, keepdims=True)
        send_e[r, 1:2] = jnp.sum(squares[of_group], axis=0, keepdims=True)
    n_first = n_row * n_x
    for dr in range(n_row):
        there = lax.rem(row + dr, n_row)
        for dx in range(n_x):
            if dr or dx:
                remote(
                    send_e.at[there],
                    recv_e.at[dr * n_x + dx - 1],
                    4,
                    {"row": there, "tp": same_plane(dx)},
                ).start()
    recv_e[n_first - 1] = send_e[row]
    wait_bytes(recv_e.at[0 : n_first - 1], recv_sem.at[4])
    summed = recv_e[0]
    for s in range(1, n_first):
        summed += recv_e[s]

    recv_g[n_near - 1] = summed
    mine = recv_g.at[n_near - 1]
    for i in range(n_near):
        remote(mine, recv_g.at[n_near + i], 6, {"grp": 1 - grp, "tp": same_column(i)}).start()
    for i in range(1, n_near):
        remote(mine, recv_g.at[i - 1], 5, {"tp": same_column(i)}).start()

    def expanded(half, first_slot):
        sums = recv_g[first_slot]
        for s in range(1, n_near):
            sums += recv_g[first_slot + s]
        norms = jnp.sum(
            jnp.where(group_lane == group_row, jnp.broadcast_to(sums[1:2], (rows, HD)), 0.0),
            axis=1,
            keepdims=True,
        )
        inverse = lax.rsqrt(norms / (n_row * n_tp * HD) + EPSILON)
        ranks = jnp.broadcast_to(sums[0:1], (rows, HD)) * inverse
        for which in range(2):
            spread_rank = jnp.where(
                lax.div(group_lane, RANK) == 2 * group_row + which, ranks, 0.0
            )
            shift = RANK
            while shift < HD:
                spread_rank += pltpu.roll(spread_rank, shift, 1)
                shift *= 2
            coefficient = jnp.where(keep, spread_rank, 0.0)[:, :picked]
            yield jnp.dot(
                coefficient.astype(BF16),
                chosen_rows[which, half * picked : (half + 1) * picked],
                preferred_element_type=F32,
            )

    wait_bytes(recv_g.at[n_near : 2 * n_near], recv_sem.at[6])
    pieces = []
    for which, delta in enumerate(expanded(0, n_near)):
        pieces += [delta[:, c * HD : (c + 1) * HD] for c in range(chunks)]
        if which:
            pieces += [jnp.zeros((rows, HD), F32)] * (-len(pieces) % stack)
        span = (early, tiles) if which else (0, early)
        for i in range(*span):
            send_f[i] = jnp.concatenate(pieces[i * stack : (i + 1) * stack], axis=0).astype(BF16)
        remote(
            send_f.at[span[0] : span[1]], recv_f.at[span[0] : span[1]], 7 + which, {"grp": 1 - grp}
        ).start()

    wait_bytes(recv_g.at[0 : n_near - 1], recv_sem.at[5])
    own = [delta.astype(BF16).astype(F32) for delta in expanded(1, 0)]
    outs = (gate_out, up_out)
    for which in range(2):
        for c in range(chunks):
            at = which * chunks + c
            if at == 0:
                wait_bytes(recv_f.at[0:early], recv_sem.at[7])
            if at == early * stack:
                wait_bytes(recv_f.at[early:tiles], recv_sem.at[8])
            other = recv_f[at // stack].astype(F32)[at % stack * rows : (at % stack + 1) * rows]
            columns = slice(c * HD, (c + 1) * HD)
            outs[which][:, columns] = (own[which][:, columns] + other).astype(BF16)

    wait_bytes(recv_b.at[0 : n_tp - 1], send_sem.at[0])
    wait_bytes(recv_st.at[0 : n_tp - 1], send_sem.at[1])
    wait_bytes(recv_c.at[0 : n_row - 1], send_sem.at[2])
    wait_bytes(recv_d.at[0 : n_tp - 1], send_sem.at[3])
    wait_bytes(recv_e.at[0 : n_first - 1], send_sem.at[4])
    wait_bytes(recv_g.at[0 : n_near - 1], send_sem.at[5])
    wait_bytes(recv_g.at[n_near : 2 * n_near], send_sem.at[6])
    wait_bytes(send_f.at[0:early], send_sem.at[7])
    wait_bytes(send_f.at[early:tiles], send_sem.at[8])


def hand_over(stream, gate, up, stream_out, gate_out, up_out, sem):
    copies = [
        pltpu.make_async_copy(source, target, sem.at[i])
        for i, (source, target) in enumerate(((stream, stream_out), (gate, gate_out), (up, up_out)))
    ]
    for copy in copies:
        copy.start()
    for copy in copies:
        copy.wait()


def layer(
    sizes,
    query,
    cached_key_rows,
    cached_value_rows,
    row_cache_length,
    attention_output_weight,
    resid,
    feed_norm_scale,
    gate_down_weight,
    up_down_weight,
    gate_expansion_weight,
    up_expansion_weight,
    row_adapter_index,
):
    n_grp, n_row, n_tp = sizes
    rows = query.shape[0]
    heads = query.shape[1] // HD
    tile = rows * (heads // n_tp)
    columns = gate_expansion_weight.shape[1]
    n_core = min(2, n_tp // 4)
    n_x = n_tp // 4 // n_core
    stack = 16 // rows
    packed = -(-2 * (columns // HD) // stack)
    smem = pl.BlockSpec(memory_space=pltpu.SMEM)
    hbm = pl.BlockSpec(memory_space=pl.ANY)
    vmem = pl.BlockSpec(memory_space=pltpu.VMEM)
    parts = pl.pallas_call(
        functools.partial(kernel, sizes),
        out_shape=(
            pltpu.VMEM(resid.shape, BF16),
            pltpu.VMEM((rows, columns), BF16),
            pltpu.VMEM((rows, columns), BF16),
        ),
        in_specs=[smem] * 2 + [hbm] * 10,
        out_specs=(vmem,) * 3,
        scratch_shapes=[
            pltpu.VMEM(query.shape, BF16),
            pltpu.VMEM(cached_key_rows.shape, BF16),
            pltpu.VMEM(cached_value_rows.shape, BF16),
            pltpu.VMEM(attention_output_weight.shape, BF16),
            pltpu.VMEM(resid.shape, BF16),
            pltpu.VMEM(feed_norm_scale.shape, BF16),
            pltpu.VMEM((2,) + gate_down_weight.shape, BF16),
            pltpu.VMEM((2,) + gate_expansion_weight.shape, BF16),
            pltpu.VMEM((rows, heads, cached_key_rows.shape[1]), BF16),
            pltpu.VMEM((rows, heads, HD), F32),
            pltpu.VMEM((n_tp, tile, HD), F32),
            pltpu.VMEM((heads, HD), F32),
            pltpu.VMEM((n_tp * tile, HD), F32),
            pltpu.VMEM((n_tp, tile, HD), BF16),
            pltpu.VMEM((n_tp, 1, HD), F32),
            pltpu.VMEM((n_tp, tile, HD), BF16),
            pltpu.VMEM((n_tp, 1, HD), F32),
            pltpu.VMEM((n_row, tile, HD), BF16),
            pltpu.VMEM((n_tp, n_row * rows, HD), BF16),
            pltpu.VMEM((n_tp, n_row * rows, HD), BF16),
            pltpu.VMEM((n_row, 2, HD), F32),
            pltpu.VMEM((n_row * n_x, 2, HD), F32),
            pltpu.VMEM((8 * n_core, 2, HD), F32),
            pltpu.VMEM((packed, 16, HD), BF16),
            pltpu.VMEM((packed, 16, HD), BF16),
            pltpu.VMEM((2, 2 * rows * RANK, columns), BF16),
            pltpu.SemaphoreType.DMA((8,)),
            pltpu.SemaphoreType.DMA((2, rows)),
            pltpu.SemaphoreType.DMA((9,)),
            pltpu.SemaphoreType.DMA((9,)),
        ],
        compiler_params=pltpu.CompilerParams(
            collective_id=0, has_side_effects=True, vmem_limit_bytes=56 * 1024 * 1024
        ),
    )(
        row_cache_length,
        row_adapter_index,
        query,
        cached_key_rows,
        cached_value_rows,
        attention_output_weight,
        resid,
        feed_norm_scale,
        gate_down_weight,
        up_down_weight,
        gate_expansion_weight,
        up_expansion_weight,
    )
    return pl.pallas_call(
        hand_over,
        out_shape=tuple(jax.ShapeDtypeStruct(part.shape, part.dtype) for part in parts),
        in_specs=[hbm] * 3,
        out_specs=(pl.BlockSpec(memory_space=pltpu.HBM),) * 3,
        scratch_shapes=[pltpu.SemaphoreType.DMA((3,))],
            compiler_params=pltpu.CompilerParams(vmem_limit_bytes=1024 * 1024),
    )(*[pltpu.with_memory_space_constraint(p, pltpu.VMEM) for p in parts])


def solution(mesh):
    sizes = tuple(mesh.shape[axis] for axis in ("grp", "row", "tp"))
    return jax.shard_map(
        functools.partial(layer, sizes),
        mesh=mesh,
        in_specs=(
            P(("grp", "row"), None),
            P(("grp", "row"), "tp", None),
            P(("grp", "row"), "tp", None),
            P(("grp", "row")),
            P("tp", "row"),
            P("grp", ("row", "tp")),
            P(("row", "tp")),
            P(("row", "tp"), None),
            P(("row", "tp"), None),
            P("grp", "tp"),
            P("grp", "tp"),
            P(),
        ),
        out_specs=(P("grp", ("row", "tp")), P(("grp", "row"), "tp"), P(("grp", "row"), "tp")),
        check_vma=False,
    )
```

time: 49.8 us -> 42.8 us (0.86)
  local copies, waits for them, and re-layouts: 3.9 us -> 0 us
  Pallas kernels: 44.9 us -> 42.1 us
    unnamed x3 -> x0, local copies, waits for them, and re-layouts: 3.9 us -> none
    pallas_call x1 -> x2, Pallas kernels: 44.9 us -> 42.1 us  [the longest x1 41.4 us: layer(): pl.pallas_call(functools.partial(kernel, sizes), out_shape=(pltpu.VMEM(re...]
where the time goes in v2:
time: 42.8 us; the launch traced here: 42.7 us
  Pallas kernels  42.1 us (98%)
  between operations  0.64 us (1%)
    pallas_call x1, Pallas kernels, layer(): pl.pallas_call(functools.partial(kernel, sizes), out_shape=(pltpu.VMEM(re...  41.4 us

profile of v2, /device:TPU:1, one launch (start us, length us, event | category | flops | bytes accessed | tf_op | source)
XLA Modules:
  0.0 42.7 jit_solution(8486503575076686839)
XLA Ops:
  0.6 41.4 %shard_map.139 = (bf16[16,128]{1,0:T(8,128)(2,1)S(1)}, bf16[4,1664]{1,0:T(4,128)(2,1)S(1)}, bf16[4,1664]{1,0:T(4,128)(2,1)S(1)}) custom-call(s32[4]{0:T(128)} %lengths.1, s32[32]{0:T(128)} %ids.1, bf16[4,16384]{1,0:T(4,128)(2,1)} %query_hbm.1, bf16[4,256,1024]{2,1,0:T(8,128)(2,1)} %key_hbm.1, bf16[4,256,1024]{2,1,0:T(8,128)(2,1)} %value_hbm.1, ...), custom_call_target="tpu_custom_call" | custom-call | tf_op jit(solution)/shard_map/pallas_call | solution.py:485
  42.1 0.6 %shard_map.140 = (bf16[16,128]{1,0:T(8,128)(2,1)}, bf16[4,1664]{1,0:T(4,128)(2,1)}, bf16[4,1664]{1,0:T(4,128)(2,1)}) custom-call(bf16[16,128]{1,0:T(8,128)(2,1)S(1)} %get-tuple-element.6.stream, bf16[4,1664]{1,0:T(4,128)(2,1)S(1)} %get-tuple-element.7.gate, bf16[4,1664]{1,0:T(4,128)(2,1)S(1)} %get-tuple-element.8.up), custom_call_target="tpu_custom_call" | custom-call | tf_op jit(solution)/shard_map/pallas_call | solution.py:543

commit v3 on v2

--- a/solution.py
+++ b/solution.py
@@ -66,6 +66,7 @@
     kv_sem,
     send_sem,
     recv_sem,
+    answer,
 ):
     n_grp, n_row, n_tp = sizes
     rows, positions, kv_width = keys.shape
@@ -110,8 +111,16 @@
     value_copies = [
         pltpu.make_async_copy(value_hbm.at[b], values.at[b], kv_sem.at[1, b]) for b in range(rows)
     ]
-    for copy in key_copies + value_copies:
+    in_order = key_copies + value_copies
+    flying = rows + rows // 2
+    for copy in in_order[:flying]:
         copy.start()
+
+    def arrived(first, count):
+        for i in range(first, first + count):
+            in_order[i].wait()
+            if i + flying < 2 * rows:
+                in_order[i + flying].start()
 
     barrier = pltpu.get_barrier_semaphore()
 
@@ -127,13 +136,16 @@
         pl.semaphore_signal(barrier, inc=1, device_id={"tp": there}, device_id_type=MESH)
         return carry
 
-    for i in range(n_near):
-        pl.semaphore_signal(
-            barrier,
-            inc=1,
-            device_id={"grp": 1 - grp, "tp": same_column(i)},
-            device_id_type=MESH,
-        )
+    @pl.when(grp == 0)
+    def _():
+        for i in range(n_near):
+            pl.semaphore_signal(
+                barrier,
+                inc=1,
+                device_id={"grp": 1 - grp, "tp": same_column(i)},
+                device_id_type=MESH,
+            )
+
     lax.fori_loop(1, n_tp, greet, 0)
     for dr in range(1, n_row):
         for dx in range(n_x):
@@ -149,8 +161,8 @@
     position = me * positions + iota((heads, positions), 1)
     stat_lane = iota((heads, HD), 1) - rows * lax.rem(iota((heads, HD), 0), per)
     stats = jnp.zeros((heads, HD), F32)
+    arrived(0, rows)
     for b in range(rows):
-        key_copies[b].wait()
         scores = jnp.concatenate(
             [
                 lax.dot_general(
@@ -177,7 +189,22 @@
         stat_rows += stat_s[pl.ds(j, n_tp, stride=per), :]
     send_st[...] = stat_rows.reshape(n_tp, 1, HD)
 
-    pl.semaphore_wait(barrier, n_tp - 1 + (n_row - 1) * n_x + n_near)
+    within = n_tp - 1 + (n_row - 1) * n_x
+
+    @pl.when(grp == 0)
+    def _():
+        pl.semaphore_wait(barrier, within)
+
+    @pl.when(grp == 1)
+    def _():
+        pl.semaphore_wait(barrier, within + n_near)
+        for i in range(n_near):
+            pl.semaphore_signal(
+                answer,
+                inc=1,
+                device_id={"grp": 1 - grp, "tp": same_column(i)},
+                device_id_type=MESH,
+            )
 
     def remote(source, target, index, device):
         return pltpu.make_async_remote_copy(
@@ -203,7 +230,8 @@
     expand_copies = (load(gate_exp_hbm, expand.at[0], 6), load(up_exp_hbm, expand.at[1], 7))
 
     for b in range(rows):
-        value_copies[b].wait()
+        if b % 2 == 0:
+            arrived(rows + b, 2)
         weights = weights_s[b]
         for k in range(kv_heads):
             acc_s[b, k * group : (k + 1) * group, :] = jnp.dot(
@@ -375,6 +403,11 @@
 
     recv_g[n_near - 1] = summed
     mine = recv_g.at[n_near - 1]
+
+    @pl.when(grp == 0)
+    def _():
+        pl.semaphore_wait(answer, n_near)
+
     for i in range(n_near):
         remote(mine, recv_g.at[n_near + i], 6, {"grp": 1 - grp, "tp": same_column(i)}).start()
     for i in range(1, n_near):
@@ -522,6 +555,7 @@
             pltpu.SemaphoreType.DMA((2, rows)),
             pltpu.SemaphoreType.DMA((9,)),
             pltpu.SemaphoreType.DMA((9,)),
+            pltpu.SemaphoreType.REGULAR,
         ],
         compiler_params=pltpu.CompilerParams(
             collective_id=0, has_side_effects=True, vmem_limit_bytes=56 * 1024 * 1024

time: 42.8 us -> 41 us (0.958)
  Pallas kernels: 42.1 us -> 40.3 us
    pallas_call x1, Pallas kernels: 41.4 us -> 39.6 us  [layer(): pl.pallas_call(functools.partial(kernel, sizes), out_shape=(pltpu.VMEM(re...]
where the time goes in v3:
time: 41 us; the launch traced here: 40.9 us
  Pallas kernels  40.3 us (98%)
  between operations  0.64 us (2%)
    pallas_call x1, Pallas kernels, layer(): pl.pallas_call(functools.partial(kernel, sizes), out_shape=(pltpu.VMEM(re...  39.6 us

profile of v3, /device:TPU:1, one launch (start us, length us, event | category | flops | bytes accessed | tf_op | source)
XLA Modules:
  0.0 40.9 jit_solution(3859431587742023132)
XLA Ops:
  0.6 39.6 %shard_map.139 = (bf16[16,128]{1,0:T(8,128)(2,1)S(1)}, bf16[4,1664]{1,0:T(4,128)(2,1)S(1)}, bf16[4,1664]{1,0:T(4,128)(2,1)S(1)}) custom-call(s32[4]{0:T(128)} %lengths.1, s32[32]{0:T(128)} %ids.1, bf16[4,16384]{1,0:T(4,128)(2,1)} %query_hbm.1, bf16[4,256,1024]{2,1,0:T(8,128)(2,1)} %key_hbm.1, bf16[4,256,1024]{2,1,0:T(8,128)(2,1)} %value_hbm.1, ...), custom_call_target="tpu_custom_call" | custom-call | tf_op jit(solution)/shard_map/pallas_call | solution.py:518
  40.3 0.6 %shard_map.140 = (bf16[16,128]{1,0:T(8,128)(2,1)}, bf16[4,1664]{1,0:T(4,128)(2,1)}, bf16[4,1664]{1,0:T(4,128)(2,1)}) custom-call(bf16[16,128]{1,0:T(8,128)(2,1)S(1)} %get-tuple-element.6.stream, bf16[4,1664]{1,0:T(4,128)(2,1)S(1)} %get-tuple-element.7.gate, bf16[4,1664]{1,0:T(4,128)(2,1)S(1)} %get-tuple-element.8.up), custom_call_target="tpu_custom_call" | custom-call | tf_op jit(solution)/shard_map/pallas_call | solution.py:577

commit v4 on v3

--- a/solution.py
+++ b/solution.py
@@ -21,8 +21,8 @@
 
 def kernel(
     sizes,
-    lengths,
-    ids,
+    lengths_hbm,
+    ids_hbm,
     query_hbm,
     key_hbm,
     value_hbm,
@@ -36,6 +36,8 @@
     stream_out,
     gate_out,
     up_out,
+    lengths,
+    ids,
     query,
     keys,
     values,
@@ -116,6 +118,9 @@
     for copy in in_order[:flying]:
         copy.start()
 
+    lengths_copy = load(lengths_hbm, lengths, 8)
+    ids_copy = load(ids_hbm, ids, 9)
+
     def arrived(first, count):
         for i in range(first, first + count):
             in_order[i].wait()
@@ -161,6 +166,7 @@
     position = me * positions + iota((heads, positions), 1)
     stat_lane = iota((heads, HD), 1) - rows * lax.rem(iota((heads, HD), 0), per)
     stats = jnp.zeros((heads, HD), F32)
+    lengths_copy.wait()
     arrived(0, rows)
     for b in range(rows):
         scores = jnp.concatenate(
@@ -245,12 +251,14 @@
             ]
     send_b[...] = msg_s[...].reshape(n_tp, tile, HD).astype(BF16)
 
-    def send_partial(k, carry):
-        there = lax.rem(me + k, n_tp)
-        remote(send_b.at[there], recv_b.at[k - 1], 0, {"tp": there}).start()
-        return carry
-
-    lax.fori_loop(1, n_tp, send_partial, 0)
+    for turn in (3, 2, 1, 0):
+
+        def send_partial(i, carry, turn=turn):
+            there = other_plane(turn) * quarter + lax.rem(place + i, quarter)
+            remote(send_b.at[there], recv_b.at[ahead(there) - 1], 0, {"tp": there}).start()
+            return carry
+
+        lax.fori_loop(0 if turn else 1, quarter, send_partial, 0)
     recv_b[n_tp - 1] = send_b[me]
 
     wait_bytes(recv_st.at[0 : n_tp - 1], recv_sem.at[1])
@@ -305,6 +313,7 @@
             column = jnp.where(iota(shape, 0) == start + i, ids[base + i], column)
         return column
 
+    ids_copy.wait()
     micro_ids = id_column(
         grp * micro_rows, micro_rows, (micro_rows, HD), 0, jnp.zeros((micro_rows, HD), jnp.int32)
     )
@@ -385,16 +394,17 @@
         send_e[r, 0:1] = jnp.sum(ranks[of_group], axis=0, keepdims=True)
         send_e[r, 1:2] = jnp.sum(squares[of_group], axis=0, keepdims=True)
     n_first = n_row * n_x
-    for dr in range(n_row):
+    for dr, dx in sorted(
+        [(dr, dx) for dr in range(n_row) for dx in range(n_x) if dr or dx],
+        key=lambda at: -min(at[0], n_row - at[0]) - min(at[1], n_x - at[1]),
+    ):
         there = lax.rem(row + dr, n_row)
-        for dx in range(n_x):
-            if dr or dx:
-                remote(
-                    send_e.at[there],
-                    recv_e.at[dr * n_x + dx - 1],
-                    4,
-                    {"row": there, "tp": same_plane(dx)},
-                ).start()
+        remote(
+            send_e.at[there],
+            recv_e.at[dr * n_x + dx - 1],
+            4,
+            {"row": there, "tp": same_plane(dx)},
+        ).start()
     recv_e[n_first - 1] = send_e[row]
     wait_bytes(recv_e.at[0 : n_first - 1], recv_sem.at[4])
     summed = recv_e[0]
@@ -512,7 +522,6 @@
     n_x = n_tp // 4 // n_core
     stack = 16 // rows
     packed = -(-2 * (columns // HD) // stack)
-    smem = pl.BlockSpec(memory_space=pltpu.SMEM)
     hbm = pl.BlockSpec(memory_space=pl.ANY)
     vmem = pl.BlockSpec(memory_space=pltpu.VMEM)
     parts = pl.pallas_call(
@@ -522,9 +531,11 @@
             pltpu.VMEM((rows, columns), BF16),
             pltpu.VMEM((rows, columns), BF16),
         ),
-        in_specs=[smem] * 2 + [hbm] * 10,
+        in_specs=[hbm] * 12,
         out_specs=(vmem,) * 3,
         scratch_shapes=[
+            pltpu.SMEM(row_cache_length.shape, jnp.int32),
+            pltpu.SMEM(row_adapter_index.shape, jnp.int32),
             pltpu.VMEM(query.shape, BF16),
             pltpu.VMEM(cached_key_rows.shape, BF16),
             pltpu.VMEM(cached_value_rows.shape, BF16),
@@ -551,7 +562,7 @@
             pltpu.VMEM((packed, 16, HD), BF16),
             pltpu.VMEM((packed, 16, HD), BF16),
             pltpu.VMEM((2, 2 * rows * RANK, columns), BF16),
-            pltpu.SemaphoreType.DMA((8,)),
+            pltpu.SemaphoreType.DMA((10,)),
             pltpu.SemaphoreType.DMA((2, rows)),
             pltpu.SemaphoreType.DMA((9,)),
             pltpu.SemaphoreType.DMA((9,)),

time: 41 us -> 40.1 us (0.978)
  Pallas kernels: 40.3 us -> 39.4 us
    pallas_call x1, Pallas kernels: 39.6 us -> 38.8 us  [layer(): pl.pallas_call(functools.partial(kernel, sizes), out_shape=(pltpu.VMEM(re...]
where the time goes in v4:
time: 40.1 us
  Pallas kernels  39.4 us (98%)
  between operations  0.64 us (2%)
    pallas_call x1, Pallas kernels, layer(): pl.pallas_call(functools.partial(kernel, sizes), out_shape=(pltpu.VMEM(re...  38.8 us

profile of v4, /device:TPU:1, one launch (start us, length us, event | category | flops | bytes accessed | tf_op | source)
XLA Modules:
  0.0 40.1 jit_solution(565878286276089665)
XLA Ops:
  0.6 38.8 %shard_map.139 = (bf16[16,128]{1,0:T(8,128)(2,1)S(1)}, bf16[4,1664]{1,0:T(4,128)(2,1)S(1)}, bf16[4,1664]{1,0:T(4,128)(2,1)S(1)}) custom-call(s32[4]{0:T(128)} %lengths_hbm.1, s32[32]{0:T(128)} %ids_hbm.1, bf16[4,16384]{1,0:T(4,128)(2,1)} %query_hbm.1, bf16[4,256,1024]{2,1,0:T(8,128)(2,1)} %key_hbm.1, bf16[4,256,1024]{2,1,0:T(8,128)(2,1)} %value_hbm.1, ...), custom_call_target="tpu_custom_call" | custom-call | tf_op jit(solution)/shard_map/pallas_call | solution.py:527
  39.4 0.6 %shard_map.140 = (bf16[16,128]{1,0:T(8,128)(2,1)}, bf16[4,1664]{1,0:T(4,128)(2,1)}, bf16[4,1664]{1,0:T(4,128)(2,1)}) custom-call(bf16[16,128]{1,0:T(8,128)(2,1)S(1)} %get-tuple-element.6.stream, bf16[4,1664]{1,0:T(4,128)(2,1)S(1)} %get-tuple-element.7.gate, bf16[4,1664]{1,0:T(4,128)(2,1)S(1)} %get-tuple-element.8.up), custom_call_target="tpu_custom_call" | custom-call | tf_op jit(solution)/shard_map/pallas_call | solution.py:588

commit v5 on v4

--- a/solution.py
+++ b/solution.py
@@ -61,6 +61,8 @@
     send_e,
     recv_e,
     recv_g,
+    send_x,
+    recv_x,
     send_f,
     recv_f,
     chosen_rows,
@@ -143,23 +145,13 @@
 
     @pl.when(grp == 0)
     def _():
-        for i in range(n_near):
-            pl.semaphore_signal(
-                barrier,
-                inc=1,
-                device_id={"grp": 1 - grp, "tp": same_column(i)},
-                device_id_type=MESH,
-            )
+        pl.semaphore_signal(barrier, inc=1, device_id={"grp": 1 - grp}, device_id_type=MESH)
 
     lax.fori_loop(1, n_tp, greet, 0)
-    for dr in range(1, n_row):
-        for dx in range(n_x):
-            pl.semaphore_signal(
-                barrier,
-                inc=1,
-                device_id={"row": lax.rem(row + dr, n_row), "tp": same_plane(dx)},
-                device_id_type=MESH,
-            )
+    for k in range(1, n_row):
+        pl.semaphore_signal(
+            barrier, inc=1, device_id={"row": lax.rem(row + k, n_row)}, device_id_type=MESH
+        )
 
     query_copy.wait()
     head_rows = query[...].astype(F32).reshape(rows, heads, HD).astype(BF16)
@@ -195,7 +187,7 @@
         stat_rows += stat_s[pl.ds(j, n_tp, stride=per), :]
     send_st[...] = stat_rows.reshape(n_tp, 1, HD)
 
-    within = n_tp - 1 + (n_row - 1) * n_x
+    within = n_tp - 1 + n_row - 1
 
     @pl.when(grp == 0)
     def _():
@@ -203,14 +195,10 @@
 
     @pl.when(grp == 1)
     def _():
-        pl.semaphore_wait(barrier, within + n_near)
-        for i in range(n_near):
-            pl.semaphore_signal(
-                answer,
-                inc=1,
-                device_id={"grp": 1 - grp, "tp": same_column(i)},
-                device_id_type=MESH,
-            )
+        pl.semaphore_wait(barrier, within + 1)
+
+    def answer_peer():
+        pl.semaphore_signal(answer, inc=1, device_id={"grp": 1 - grp}, device_id_type=MESH)
 
     def remote(source, target, index, device):
         return pltpu.make_async_remote_copy(
@@ -280,6 +268,11 @@
     for k in range(1, n_row):
         remote(recv_c.at[row], recv_c.at[row], 2, {"row": lax.rem(row + k, n_row)}).start()
     wait_bytes(recv_c.at[0 : n_row - 1], recv_sem.at[2])
+
+    @pl.when(grp == 1)
+    def _():
+        answer_peer()
+
     gathered = recv_c[...].astype(F32)
     left = jnp.concatenate(
         [
@@ -353,6 +346,11 @@
             pick, expand[which], preferred_element_type=F32
         ).astype(BF16)
 
+    @pl.when(grp == 0)
+    def _():
+        pl.semaphore_wait(answer, 1)
+        answer_peer()
+
     resid_copy.wait()
     gain_copy.wait()
     for copy in down_copies:
@@ -393,6 +391,28 @@
         of_group = slice(r * rows, (r + 1) * rows)
         send_e[r, 0:1] = jnp.sum(ranks[of_group], axis=0, keepdims=True)
         send_e[r, 1:2] = jnp.sum(squares[of_group], axis=0, keepdims=True)
+        send_x[r] = send_e[r, 0:1]
+
+    @pl.when(grp == 1)
+    def _():
+        pl.semaphore_wait(answer, 1)
+
+    for dr in (2, 1, 3, 0):
+        to_row = lax.rem(row + dr, n_row)
+        for turn in range(4):
+
+            def send_ranks(i, carry, dr=dr, to_row=to_row, turn=turn):
+                there = other_plane(turn) * quarter + lax.rem(place + quarter // 2 + i, quarter)
+                remote(
+                    send_x.at[to_row],
+                    recv_x.at[dr * n_tp + ahead(there)],
+                    6,
+                    {"grp": 1 - grp, "row": to_row, "tp": there},
+                ).start()
+                return carry
+
+            lax.fori_loop(0, quarter, send_ranks, 0)
+
     n_first = n_row * n_x
     for dr, dx in sorted(
         [(dr, dx) for dr in range(n_row) for dx in range(n_x) if dr or dx],
@@ -412,28 +432,10 @@
         summed += recv_e[s]
 
     recv_g[n_near - 1] = summed
-    mine = recv_g.at[n_near - 1]
-
-    @pl.when(grp == 0)
-    def _():
-        pl.semaphore_wait(answer, n_near)
-
-    for i in range(n_near):
-        remote(mine, recv_g.at[n_near + i], 6, {"grp": 1 - grp, "tp": same_column(i)}).start()
     for i in range(1, n_near):
-        remote(mine, recv_g.at[i - 1], 5, {"tp": same_column(i)}).start()
-
-    def expanded(half, first_slot):
-        sums = recv_g[first_slot]
-        for s in range(1, n_near):
-            sums += recv_g[first_slot + s]
-        norms = jnp.sum(
-            jnp.where(group_lane == group_row, jnp.broadcast_to(sums[1:2], (rows, HD)), 0.0),
-            axis=1,
-            keepdims=True,
-        )
-        inverse = lax.rsqrt(norms / (n_row * n_tp * HD) + EPSILON)
-        ranks = jnp.broadcast_to(sums[0:1], (rows, HD)) * inverse
+        remote(recv_g.at[n_near - 1], recv_g.at[i - 1], 5, {"tp": same_column(i)}).start()
+
+    def expanded(half, ranks):
         for which in range(2):
             spread_rank = jnp.where(
                 lax.div(group_lane, RANK) == 2 * group_row + which, ranks, 0.0
@@ -449,9 +451,18 @@
                 preferred_element_type=F32,
             )
 
-    wait_bytes(recv_g.at[n_near : 2 * n_near], recv_sem.at[6])
+    def added(ref, count):
+        chains = [ref[s] for s in range(8)]
+        for s in range(8, count):
+            chains[s % 8] += ref[s]
+        while len(chains) > 1:
+            chains = [low + high for low, high in zip(chains[::2], chains[1::2])]
+        return chains[0]
+
+    wait_bytes(recv_x, recv_sem.at[6])
+    other_ranks = jnp.broadcast_to(added(recv_x, n_row * n_tp), (rows, HD))
     pieces = []
-    for which, delta in enumerate(expanded(0, n_near)):
+    for which, delta in enumerate(expanded(0, other_ranks)):
         pieces += [delta[:, c * HD : (c + 1) * HD] for c in range(chunks)]
         if which:
             pieces += [jnp.zeros((rows, HD), F32)] * (-len(pieces) % stack)
@@ -463,7 +474,17 @@
         ).start()
 
     wait_bytes(recv_g.at[0 : n_near - 1], recv_sem.at[5])
-    own = [delta.astype(BF16).astype(F32) for delta in expanded(1, 0)]
+    sums = recv_g[0]
+    for s in range(1, n_near):
+        sums += recv_g[s]
+    norms = jnp.sum(
+        jnp.where(group_lane == group_row, jnp.broadcast_to(sums[1:2], (rows, HD)), 0.0),
+        axis=1,
+        keepdims=True,
+    )
+    inverse = lax.rsqrt(norms / (n_row * n_tp * HD) + EPSILON)
+    own_ranks = jnp.broadcast_to(sums[0:1], (rows, HD)) * inverse
+    own = [delta.astype(BF16).astype(F32) for delta in expanded(1, own_ranks)]
     outs = (gate_out, up_out)
     for which in range(2):
         for c in range(chunks):
@@ -474,7 +495,7 @@
                 wait_bytes(recv_f.at[early:tiles], recv_sem.at[8])
             other = recv_f[at // stack].astype(F32)[at % stack * rows : (at % stack + 1) * rows]
             columns = slice(c * HD, (c + 1) * HD)
-            outs[which][:, columns] = (own[which][:, columns] + other).astype(BF16)
+            outs[which][:, columns] = (own[which][:, columns] + other * inverse).astype(BF16)
 
     wait_bytes(recv_b.at[0 : n_tp - 1], send_sem.at[0])
     wait_bytes(recv_st.at[0 : n_tp - 1], send_sem.at[1])
@@ -482,7 +503,7 @@
     wait_bytes(recv_d.at[0 : n_tp - 1], send_sem.at[3])
     wait_bytes(recv_e.at[0 : n_first - 1], send_sem.at[4])
     wait_bytes(recv_g.at[0 : n_near - 1], send_sem.at[5])
-    wait_bytes(recv_g.at[n_near : 2 * n_near], send_sem.at[6])
+    wait_bytes(recv_x, send_sem.at[6])
     wait_bytes(send_f.at[0:early], send_sem.at[7])
     wait_bytes(send_f.at[early:tiles], send_sem.at[8])
 
@@ -558,7 +579,9 @@
             pltpu.VMEM((n_tp, n_row * rows, HD), BF16),
             pltpu.VMEM((n_row, 2, HD), F32),
             pltpu.VMEM((n_row * n_x, 2, HD), F32),
-            pltpu.VMEM((8 * n_core, 2, HD), F32),
+            pltpu.VMEM((4 * n_core, 2, HD), F32),
+            pltpu.VMEM((n_row, 1, HD), F32),
+            pltpu.VMEM((n_row * n_tp, 1, HD), F32),
             pltpu.VMEM((packed, 16, HD), BF16),
             pltpu.VMEM((packed, 16, HD), BF16),
             pltpu.VMEM((2, 2 * rows * RANK, columns), BF16),

time: 40.1 us -> 38.6 us (0.963)
  Pallas kernels: 39.4 us -> 37.9 us
    pallas_call x1, Pallas kernels: 38.8 us -> 37.2 us  [layer(): pl.pallas_call(functools.partial(kernel, sizes), out_shape=(pltpu.VMEM(re...]
where the time goes in v5:
time: 38.6 us; the launch traced here: 38.5 us
  Pallas kernels  37.9 us (98%)
  between operations  0.64 us (2%)
    pallas_call x1, Pallas kernels, layer(): pl.pallas_call(functools.partial(kernel, sizes), out_shape=(pltpu.VMEM(re...  37.2 us

profile of v5, /device:TPU:1, one launch (start us, length us, event | category | flops | bytes accessed | tf_op | source)
XLA Modules:
  0.0 38.5 jit_solution(17356311297475524245)
XLA Ops:
  0.6 37.2 %shard_map.139 = (bf16[16,128]{1,0:T(8,128)(2,1)S(1)}, bf16[4,1664]{1,0:T(4,128)(2,1)S(1)}, bf16[4,1664]{1,0:T(4,128)(2,1)S(1)}) custom-call(s32[4]{0:T(128)} %lengths_hbm.1, s32[32]{0:T(128)} %ids_hbm.1, bf16[4,16384]{1,0:T(4,128)(2,1)} %query_hbm.1, bf16[4,256,1024]{2,1,0:T(8,128)(2,1)} %key_hbm.1, bf16[4,256,1024]{2,1,0:T(8,128)(2,1)} %value_hbm.1, ...), custom_call_target="tpu_custom_call" | custom-call | tf_op jit(solution)/shard_map/pallas_call | solution.py:548
  37.9 0.6 %shard_map.140 = (bf16[16,128]{1,0:T(8,128)(2,1)}, bf16[4,1664]{1,0:T(4,128)(2,1)}, bf16[4,1664]{1,0:T(4,128)(2,1)}) custom-call(bf16[16,128]{1,0:T(8,128)(2,1)S(1)} %get-tuple-element.6.stream, bf16[4,1664]{1,0:T(4,128)(2,1)S(1)} %get-tuple-element.7.gate, bf16[4,1664]{1,0:T(4,128)(2,1)S(1)} %get-tuple-element.8.up), custom_call_target="tpu_custom_call" | custom-call | tf_op jit(solution)/shard_map/pallas_call | solution.py:611

commit v6 on v5

--- a/solution.py
+++ b/solution.py
@@ -108,6 +108,14 @@
     def ahead(there):
         return lax.rem(there - me + n_tp, n_tp)
 
+    def added(terms):
+        chains = terms[:4]
+        for at, term in enumerate(terms[4:]):
+            chains[at % 4] += term
+        while len(chains) > 1:
+            chains = [low + high for low, high in zip(chains[::2], chains[1::2])]
+        return chains[0]
+
     query_copy = load(query_hbm, query, 0)
     key_copies = [
         pltpu.make_async_copy(key_hbm.at[b], keys.at[b], kv_sem.at[0, b]) for b in range(rows)
@@ -193,12 +201,15 @@
     def _():
         pl.semaphore_wait(barrier, within)
 
+    def answer_peer(which):
+        pl.semaphore_signal(
+            answer.at[which], inc=1, device_id={"grp": 1 - grp}, device_id_type=MESH
+        )
+
     @pl.when(grp == 1)
     def _():
         pl.semaphore_wait(barrier, within + 1)
-
-    def answer_peer():
-        pl.semaphore_signal(answer, inc=1, device_id={"grp": 1 - grp}, device_id_type=MESH)
+        answer_peer(0)
 
     def remote(source, target, index, device):
         return pltpu.make_async_remote_copy(
@@ -217,12 +228,6 @@
 
     lax.fori_loop(1, n_tp, send_stats, 0)
     recv_st[n_tp - 1] = send_st[me]
-    wo_copy = load(wo_hbm, wo, 1)
-    resid_copy = load(resid_hbm, resid, 2)
-    gain_copy = load(gain_hbm, gain, 3)
-    down_copies = (load(gate_down_hbm, down.at[0], 4), load(up_down_hbm, down.at[1], 5))
-    expand_copies = (load(gate_exp_hbm, expand.at[0], 6), load(up_exp_hbm, expand.at[1], 7))
-
     for b in range(rows):
         if b % 2 == 0:
             arrived(rows + b, 2)
@@ -247,6 +252,11 @@
             return carry
 
         lax.fori_loop(0 if turn else 1, quarter, send_partial, 0)
+    wo_copy = load(wo_hbm, wo, 1)
+    resid_copy = load(resid_hbm, resid, 2)
+    gain_copy = load(gain_hbm, gain, 3)
+    down_copies = (load(gate_down_hbm, down.at[0], 4), load(up_down_hbm, down.at[1], 5))
+    expand_copies = (load(gate_exp_hbm, expand.at[0], 6), load(up_exp_hbm, expand.at[1], 7))
     recv_b[n_tp - 1] = send_b[me]
 
     wait_bytes(recv_st.at[0 : n_tp - 1], recv_sem.at[1])
@@ -260,18 +270,18 @@
     for s in range(n_tp):
         share_s[s] = jnp.broadcast_to(share[:, s : s + 1], (tile, HD))
     wait_bytes(recv_b.at[0 : n_tp - 1], recv_sem.at[0])
-    attended = share_s[0] * recv_b[0].astype(F32)
-    for s in range(1, n_tp):
-        attended += share_s[s] * recv_b[s].astype(F32)
+    attended = added([share_s[s] * recv_b[s].astype(F32) for s in range(n_tp)])
 
     recv_c[row] = attended.astype(BF16)
     for k in range(1, n_row):
         remote(recv_c.at[row], recv_c.at[row], 2, {"row": lax.rem(row + k, n_row)}).start()
     wait_bytes(recv_c.at[0 : n_row - 1], recv_sem.at[2])
 
-    @pl.when(grp == 1)
+    @pl.when(grp == 0)
     def _():
-        answer_peer()
+        pl.semaphore_wait(answer.at[0], 1)
+
+    answer_peer(1)
 
     gathered = recv_c[...].astype(F32)
     left = jnp.concatenate(
@@ -312,21 +322,20 @@
     )
     lane_adapter = lax.div(iota((micro_rows, HD), 1), RANK)
     half_adapters = expand.shape[1] // RANK
-    picked = rows * RANK
+    picked = 2 * rows * RANK
     group_row = iota((rows, HD), 0)
     group_lane = iota((rows, HD), 1)
     chunks = expand.shape[2] // HD
     stack = recv_f.shape[1] // rows
     tiles = recv_f.shape[0]
     early = chunks // stack
-    keep = lax.div(group_lane, RANK) == group_row
     wanted = jnp.zeros((2 * picked, HD), jnp.int32)
     pick_row = iota((2 * picked, HD), 0)
     for half in range(2):
         of_grp = 1 - grp if half == 0 else grp
         for i in range(rows):
             wanted = jnp.where(
-                lax.div(pick_row, RANK) == half * rows + i,
+                lax.div(pick_row, 2 * RANK) == half * rows + i,
                 ids[of_grp * micro_rows + row * rows + i],
                 wanted,
             )
@@ -346,21 +355,13 @@
             pick, expand[which], preferred_element_type=F32
         ).astype(BF16)
 
-    @pl.when(grp == 0)
-    def _():
-        pl.semaphore_wait(answer, 1)
-        answer_peer()
-
     resid_copy.wait()
     gain_copy.wait()
     for copy in down_copies:
         copy.wait()
     wait_bytes(recv_d.at[0 : n_tp - 1], recv_sem.at[3])
     hidden = resid[...].astype(F32)
-    projected = recv_d[0].astype(F32)
-    for s in range(1, n_tp):
-        projected += recv_d[s].astype(F32)
-    hidden = hidden + projected
+    hidden = hidden + added([recv_d[s].astype(F32) for s in range(n_tp)])
     stream_out[...] = hidden.astype(BF16)
     squares = jnp.sum(hidden * hidden, axis=1, keepdims=True)
     scaled = (hidden * gain[...].astype(F32).reshape(1, HD)).astype(BF16)
@@ -393,26 +394,6 @@
         send_e[r, 1:2] = jnp.sum(squares[of_group], axis=0, keepdims=True)
         send_x[r] = send_e[r, 0:1]
 
-    @pl.when(grp == 1)
-    def _():
-        pl.semaphore_wait(answer, 1)
-
-    for dr in (2, 1, 3, 0):
-        to_row = lax.rem(row + dr, n_row)
-        for turn in range(4):
-
-            def send_ranks(i, carry, dr=dr, to_row=to_row, turn=turn):
-                there = other_plane(turn) * quarter + lax.rem(place + quarter // 2 + i, quarter)
-                remote(
-                    send_x.at[to_row],
-                    recv_x.at[dr * n_tp + ahead(there)],
-                    6,
-                    {"grp": 1 - grp, "row": to_row, "tp": there},
-                ).start()
-                return carry
-
-            lax.fori_loop(0, quarter, send_ranks, 0)
-
     n_first = n_row * n_x
     for dr, dx in sorted(
         [(dr, dx) for dr in range(n_row) for dx in range(n_x) if dr or dx],
@@ -425,11 +406,28 @@
             4,
             {"row": there, "tp": same_plane(dx)},
         ).start()
+
+    pl.semaphore_wait(answer.at[1], 1)
+
+    for turn, dr in ((0, 2), (0, 1), (0, 3), (1, 2), (1, 1), (1, 3), (0, 0), (3, 2),
+                     (2, 2), (3, 1), (3, 3), (2, 1), (2, 3), (1, 0), (3, 0), (2, 0)):
+        to_row = lax.rem(row + dr, n_row)
+
+        def send_ranks(i, carry, dr=dr, to_row=to_row, turn=turn):
+            there = other_plane(turn) * quarter + lax.rem(place + quarter // 2 + i, quarter)
+            remote(
+                send_x.at[to_row],
+                recv_x.at[dr * n_tp + ahead(there)],
+                6,
+                {"grp": 1 - grp, "row": to_row, "tp": there},
+            ).start()
+            return carry
+
+        lax.fori_loop(0, quarter, send_ranks, 0)
+
     recv_e[n_first - 1] = send_e[row]
     wait_bytes(recv_e.at[0 : n_first - 1], recv_sem.at[4])
-    summed = recv_e[0]
-    for s in range(1, n_first):
-        summed += recv_e[s]
+    summed = added([recv_e[s] for s in range(n_first)])
 
     recv_g[n_near - 1] = summed
     for i in range(1, n_near):
@@ -437,30 +435,15 @@
 
     def expanded(half, ranks):
         for which in range(2):
-            spread_rank = jnp.where(
-                lax.div(group_lane, RANK) == 2 * group_row + which, ranks, 0.0
-            )
-            shift = RANK
-            while shift < HD:
-                spread_rank += pltpu.roll(spread_rank, shift, 1)
-                shift *= 2
-            coefficient = jnp.where(keep, spread_rank, 0.0)[:, :picked]
+            mine = lax.div(group_lane, RANK) == 2 * group_row + which
             yield jnp.dot(
-                coefficient.astype(BF16),
+                jnp.where(mine, ranks, 0.0).astype(BF16),
                 chosen_rows[which, half * picked : (half + 1) * picked],
                 preferred_element_type=F32,
             )
 
-    def added(ref, count):
-        chains = [ref[s] for s in range(8)]
-        for s in range(8, count):
-            chains[s % 8] += ref[s]
-        while len(chains) > 1:
-            chains = [low + high for low, high in zip(chains[::2], chains[1::2])]
-        return chains[0]
-
     wait_bytes(recv_x, recv_sem.at[6])
-    other_ranks = jnp.broadcast_to(added(recv_x, n_row * n_tp), (rows, HD))
+    other_ranks = jnp.broadcast_to(added([recv_x[s] for s in range(n_row * n_tp)]), (rows, HD))
     pieces = []
     for which, delta in enumerate(expanded(0, other_ranks)):
         pieces += [delta[:, c * HD : (c + 1) * HD] for c in range(chunks)]
@@ -474,9 +457,7 @@
         ).start()
 
     wait_bytes(recv_g.at[0 : n_near - 1], recv_sem.at[5])
-    sums = recv_g[0]
-    for s in range(1, n_near):
-        sums += recv_g[s]
+    sums = added([recv_g[s] for s in range(n_near)])
     norms = jnp.sum(
         jnp.where(group_lane == group_row, jnp.broadcast_to(sums[1:2], (rows, HD)), 0.0),
         axis=1,
@@ -584,12 +565,12 @@
             pltpu.VMEM((n_row * n_tp, 1, HD), F32),
             pltpu.VMEM((packed, 16, HD), BF16),
             pltpu.VMEM((packed, 16, HD), BF16),
-            pltpu.VMEM((2, 2 * rows * RANK, columns), BF16),
+            pltpu.VMEM((2, 4 * rows * RANK, columns), BF16),
             pltpu.SemaphoreType.DMA((10,)),
             pltpu.SemaphoreType.DMA((2, rows)),
             pltpu.SemaphoreType.DMA((9,)),
             pltpu.SemaphoreType.DMA((9,)),
-            pltpu.SemaphoreType.REGULAR,
+            pltpu.SemaphoreType.REGULAR((2,)),
         ],
         compiler_params=pltpu.CompilerParams(
             collective_id=0, has_side_effects=True, vmem_limit_bytes=56 * 1024 * 1024

time: 38.6 us -> 38.5 us (level); the launches traced: 38.5 us -> 37.9 us
  Pallas kernels: 37.9 us -> 37.3 us
    pallas_call x1, Pallas kernels: 37.2 us -> 36.7 us  [layer(): pl.pallas_call(functools.partial(kernel, sizes), out_shape=(pltpu.VMEM(re...]
where the time goes in v6:
time: 38.5 us; the launch traced here: 37.9 us
  Pallas kernels  37.3 us (97%)
  between operations  0.64 us (2%)
    pallas_call x1, Pallas kernels, layer(): pl.pallas_call(functools.partial(kernel, sizes), out_shape=(pltpu.VMEM(re...  36.7 us

profile of v6, /device:TPU:1, one launch (start us, length us, event | category | flops | bytes accessed | tf_op | source)
XLA Modules:
  0.0 37.9 jit_solution(13699339050488949651)
XLA Ops:
  0.6 36.7 %shard_map.139 = (bf16[16,128]{1,0:T(8,128)(2,1)S(1)}, bf16[4,1664]{1,0:T(4,128)(2,1)S(1)}, bf16[4,1664]{1,0:T(4,128)(2,1)S(1)}) custom-call(s32[4]{0:T(128)} %lengths_hbm.1, s32[32]{0:T(128)} %ids_hbm.1, bf16[4,16384]{1,0:T(4,128)(2,1)} %query_hbm.1, bf16[4,256,1024]{2,1,0:T(8,128)(2,1)} %key_hbm.1, bf16[4,256,1024]{2,1,0:T(8,128)(2,1)} %value_hbm.1, ...), custom_call_target="tpu_custom_call" | custom-call | tf_op jit(solution)/shard_map/pallas_call | solution.py:529
  37.3 0.6 %shard_map.140 = (bf16[16,128]{1,0:T(8,128)(2,1)}, bf16[4,1664]{1,0:T(4,128)(2,1)}, bf16[4,1664]{1,0:T(4,128)(2,1)}) custom-call(bf16[16,128]{1,0:T(8,128)(2,1)S(1)} %get-tuple-element.6.stream, bf16[4,1664]{1,0:T(4,128)(2,1)S(1)} %get-tuple-element.7.gate, bf16[4,1664]{1,0:T(4,128)(2,1)S(1)} %get-tuple-element.8.up), custom_call_target="tpu_custom_call" | custom-call | tf_op jit(solution)/shard_map/pallas_call | solution.py:592
